TPU v7x, 32 devices: a whole 2x2x4 slice. The times are simulated.
32 devices in a mesh: rows: 4 (over y, core), chan: 8 (over z, x).
Axes of the slice: x: 2, y: 2, z: 4, core: 2. Of those that a mesh axis runs over, the one named last changes fastest.
Arguments:
- activations: bfloat16 [5120, 1536], P(('rows', 'chan')), may hold values from -6 to 6
- condition: bfloat16 [8, 1536], P('rows'), may hold values from -6 to 6
- seq_lengths: int32 [4, 2], P('rows'), may hold values from 1 to 1024, 1280 in all within a row
- w_ada: bfloat16 [3, 1536, 1536], P(None, 'chan'), may hold values from -0.15625 to 0.15625
- b_ada: float32 [3, 1536], P(None, 'chan'), may hold values from -3 to 3
- norm_gain: float32 [1536], P('chan'), may hold values from 0.25 to 1.75
- w_in_x: bfloat16 [3072, 1536], P('chan'), may hold values from -0.15625 to 0.15625
- w_in_z: bfloat16 [3072, 1536], P('chan'), may hold values from -0.15625 to 0.15625
- conv_weight: float32 [3072, 4], P('chan'), may hold values from -3 to 3
- conv_bias: float32 [3072], P('chan'), may hold values from -1 to 1
- w_xproj: bfloat16 [3072, 128], P('chan'), may hold values from -0.109375 to 0.109375
- w_dt: bfloat16 [96, 3072], P(None, 'chan'), may hold values from -0.625 to 0.625
- dt_bias: float32 [3072], P('chan'), may hold values from -6.9 to -2.3
- a_log: float32 [3072, 16], P('chan'), may hold values from 0 to 2.77
- d_skip: float32 [3072], P('chan'), may hold values from 0.5 to 1.5
- w_out: bfloat16 [3072, 1536], P('chan'), may hold values from -0.3125 to 0.3125
- grad_out: bfloat16 [5120, 1536], P(('rows', 'chan')), may hold values from -6 to 6
Outputs:
- block_out: bfloat16 [5120, 1536], P(('rows', 'chan'))
- grad_input: bfloat16 [5120, 1536], P(('rows', 'chan'))
- grad_w_ada: float32 [3, 1536, 1536], P(None, 'chan')
- grad_b_ada: float32 [3, 1536], P(None, 'chan')
- grad_gain: float32 [1536], P('chan')
- grad_w_in_x: float32 [3072, 1536], P('chan')
- grad_w_in_z: float32 [3072, 1536], P('chan')
- grad_conv_weight: float32 [3072, 4], P('chan')
- grad_conv_bias: float32 [3072], P('chan')
- grad_w_xproj: float32 [3072, 128], P('chan')
- grad_w_dt: float32 [96, 3072], P(None, 'chan')
- grad_dt_bias: float32 [3072], P('chan')
- grad_a_log: float32 [3072, 16], P('chan')
- grad_d_skip: float32 [3072], P('chan')
- grad_w_out: float32 [3072, 1536], P('chan')
Inputs may be any that keep to these rules, and one draw needn't show every extreme that they name: `seq_lengths`: row r lists, in order, the lengths of the 2 sequences packed into the 1280 tokens of index r of rows; they sum to 1280.
All inputs are finite; a program needn't handle non-finite values.
Results may differ from a plain program's by a relative error of at most 0.012.
The roundings to bfloat16 on the way count: a program that leaves them out, or rounds other values in their place, can miss the bound.
Values may be sent and summed in bfloat16 or wider, within the bound.
No kernel may reach another device: no remote copies, remote signals or barrier semaphores. Data moves between devices by JAX's collectives and lax.ppermute only.
A program may use at most 576 MiB of HBM per device.

v0:
```python
import functools, math
import jax, jax.numpy as jnp
from jax import lax
from jax.experimental import pallas as pl
from jax.experimental.pallas import tpu as pltpu
from jax.sharding import PartitionSpec as P
CHUNK=16
LOG2E=math.log2(math.e)
f32=jnp.float32; bf16=jnp.bfloat16

def scan_kernel(n_seq, row_mode, begins_ref, delta_ref, act_ref, dm_ref, an_ref, bt_ref, ct_ref, cblk_ref, bblk_ref,
                y_ref, dd_ref, da_ref, ga_ref, dbm_ref, dcm_ref, pf_s, db_s, drv_b, both_b, dd_b, de_b, darow_s):
    T, C = delta_ref.shape
    N = an_ref.shape[0]
    n_chunks = T // CHUNK
    an = an_ref[...]
    a2 = an * LOG2E

    def rows(ref, t):
        if row_mode == 0:
            return ref[pl.ds(t, 1), :]
        half = ref[pl.ds(t, 8, stride=0), :]
        return jnp.concatenate([half, half], axis=0)

    def prep(c):
        base = pl.multiple_of(c * CHUNK, CHUNK)
        darow_s[...] = delta_ref[pl.ds(base, CHUNK), :] * act_ref[pl.ds(base, CHUNK), :].astype(f32)
        return base

    def has_start(base, shift):
        hit = False
        for s in range(1, n_seq):
            at = begins_ref[0, s] - shift
            here = (at >= base) & (at < base + CHUNK)
            hit = here if hit is False else (hit | here)
        return hit

    def keep_at(t, shift):
        keep = None
        for s in range(1, n_seq):
            k = jnp.where(begins_ref[0, s] - shift == t, 0.0, 1.0).astype(f32)
            keep = k if keep is None else keep * k
        return keep

    def forward(c, carry):
        base = prep(c)
        bt = bt_ref[c]
        ct = ct_ref[c]

        def run(masked, sf, g):
            for i in range(CHUNK):
                decay = jnp.exp2(rows(delta_ref, base + i) * a2)
                drive = rows(darow_s, i) * bt[:, i : i + 1]
                if masked:
                    keep = keep_at(base + i, 0)
                    sf = sf * keep
                    g = g * keep
                pf = decay * sf
                sf = pf + drive
                db = rows(dm_ref, base + i) * ct[:, i : i + 1] + g
                g = decay * db
                at = pl.multiple_of(base * N + i * N, N)
                pf_s[pl.ds(at, N), :] = pf
                db_s[pl.ds(at, N), :] = db
            return sf, g

        if n_seq == 1:
            return run(False, *carry)
        return lax.cond(has_start(base, 0), functools.partial(run, True), functools.partial(run, False), *carry)

    zero = jnp.zeros((N, C), f32)
    lax.fori_loop(0, n_chunks, forward, (zero, zero))
    tile = pl.program_id(0)
    r = lax.broadcasted_iota(jnp.int32, (CHUNK, CHUNK * N), 0)
    q = lax.broadcasted_iota(jnp.int32, (CHUNK, CHUNK * N), 1) // N
    diag = (r == q).astype(f32)
    ones_blk = diag.astype(bf16)

    def backward(k, carry):
        c = n_chunks - 1 - k
        base = prep(c)
        bt = bt_ref[c]
        ct = ct_ref[c]

        def run(masked, sb, g, ga):
            for i in range(CHUNK - 1, -1, -1):
                drow = rows(delta_ref, base + i)
                decay = jnp.exp2(drow * a2)
                drive = rows(darow_s, i) * bt[:, i : i + 1]
                if masked:
                    keep = keep_at(base + i, 1)
                    sb = sb * keep
                    g = g * keep
                pb = decay * sb
                sb = pb + drive
                df = rows(dm_ref, base + i) * ct[:, i : i + 1] + g
                g = decay * df
                at = pl.multiple_of(base * N + i * N, N)
                pf = pf_s[pl.ds(at, N), :]
                db = db_s[pl.ds(at, N), :]
                d_expo = df * pf + db * pb
                ga = ga + d_expo * drow
                both_b[i * N : (i + 1) * N, :] = (pf + drive + sb).astype(bf16)
                dd_b[i * N : (i + 1) * N, :] = (df + db).astype(bf16)
                de_b[i * N : (i + 1) * N, :] = (d_expo * an).astype(bf16)
            return sb, g, ga

        if n_seq == 1:
            carry = run(False, *carry)
        else:
            carry = lax.cond(has_start(base, 1), functools.partial(run, True), functools.partial(run, False), *carry)
        here = pl.ds(base, CHUNK)
        both = both_b[...]
        ddv = dd_b[...]
        y_ref[here, :] = jnp.dot(cblk_ref[here, :], both, preferred_element_type=f32)
        through = jnp.dot(bblk_ref[here, :], ddv, preferred_element_type=f32)
        expo = jnp.dot(ones_blk, de_b[...], preferred_element_type=f32)
        delta = delta_ref[here, :]
        dd_ref[here, :] = expo + through * act_ref[here, :].astype(f32)
        da_ref[here, :] = through * delta
        tdot = functools.partial(lax.dot_general, dimension_numbers=(((1,), (1,)), ((), ())), preferred_element_type=f32)
        dcm = jnp.sum(tdot(dm_ref[here, :].astype(bf16), both) * diag, axis=0, keepdims=True)
        dbm = jnp.sum(tdot(darow_s[...].astype(bf16), ddv) * diag, axis=0, keepdims=True)

        @pl.when(tile == 0)
        def _():
            dcm_ref[pl.ds(c, 1), :] = dcm
            dbm_ref[pl.ds(c, 1), :] = dbm

        @pl.when(tile != 0)
        def _():
            dcm_ref[pl.ds(c, 1), :] += dcm
            dbm_ref[pl.ds(c, 1), :] += dbm

        return carry

    _, _, ga = lax.fori_loop(0, n_chunks, backward, (zero, zero, zero))
    ga_ref[...] = ga


def scans(deltas, act_low, d_mixed, a_neg, b_mat, c_mat, begins, row_mode=0):
    T, C = deltas.shape
    N = a_neg.shape[0]
    tile = 128 if C % 128 == 0 else C
    n_tiles = C // tile
    n_chunks = T // CHUNK
    bt = b_mat.reshape(n_chunks, CHUNK, N).transpose(0, 2, 1)
    ct = c_mat.reshape(n_chunks, CHUNK, N).transpose(0, 2, 1)
    same = (jnp.arange(T)[:, None] % CHUNK == jnp.arange(CHUNK * N)[None, :] // N)
    blk = lambda m: jnp.where(same, jnp.tile(m, (1, CHUNK)), 0.0).astype(bf16)
    col = lambda: pl.BlockSpec((T, tile), lambda j: (0, j))
    fix = lambda shape: pl.BlockSpec(shape, lambda j: (0,) * len(shape))
    sds = jax.ShapeDtypeStruct
    out = pl.pallas_call(
        functools.partial(scan_kernel, begins.shape[1], row_mode),
        grid=(n_tiles,),
        in_specs=[pl.BlockSpec(memory_space=pltpu.SMEM), col(), col(), col(), pl.BlockSpec((N, tile), lambda j: (0, j)),
                  fix(bt.shape), fix(ct.shape), fix((T, CHUNK * N)), fix((T, CHUNK * N))],
        out_specs=[col(), col(), col(), pl.BlockSpec((N, tile), lambda j: (0, j)), fix((n_chunks, CHUNK * N)), fix((n_chunks, CHUNK * N))],
        out_shape=[sds((T, C), f32), sds((T, C), f32), sds((T, C), f32), sds((N, C), f32),
                   sds((n_chunks, CHUNK * N), f32), sds((n_chunks, CHUNK * N), f32)],
        scratch_shapes=[pltpu.VMEM((T * N, tile), f32), pltpu.VMEM((T * N, tile), f32), pltpu.VMEM((CHUNK, tile), f32),
                        pltpu.VMEM((CHUNK * N, tile), bf16), pltpu.VMEM((CHUNK * N, tile), bf16), pltpu.VMEM((CHUNK * N, tile), bf16),
                        pltpu.VMEM((CHUNK, tile), f32)],
        compiler_params=pltpu.CompilerParams(vmem_limit_bytes=56 * 2**20, dimension_semantics=("arbitrary",)),
        cost_estimate=pl.CostEstimate(flops=T * C * N * 60, bytes_accessed=T * C * 24, transcendentals=2 * T * C * N),
        name="scan_all",
    )(begins, deltas, act_low, d_mixed, a_neg, bt, ct, blk(c_mat), blk(b_mat))
    y, dd, da, ga, dbm, dcm = out
    return y, dd, da, ga, dbm.reshape(T, N), dcm.reshape(T, N)


EPSILON = 1e-06
HIGHEST = lax.Precision.HIGHEST


def low_dot(left, right):
    return jnp.dot(left, right, preferred_element_type=f32)


def dot_across(left, right):
    return lax.dot_general(left, right, (((1,), (1,)), ((), ())), preferred_element_type=f32)


def dot_tokens(left, right):
    return lax.dot_general(left, right, (((0,), (0,)), ((), ())), preferred_element_type=f32)


def delay_rows(operand, lag):
    if lag == 0:
        return operand
    padding = jnp.zeros((lag,) + operand.shape[1:], operand.dtype)
    return jnp.concatenate([padding, operand[:-lag]], axis=0)


def advance_rows(operand, lag):
    if lag == 0:
        return operand
    padding = jnp.zeros((lag,) + operand.shape[1:], operand.dtype)
    return jnp.concatenate([operand[lag:], padding], axis=0)


def silu_slope(operand):
    squash = jax.nn.sigmoid(operand)
    return squash * (1.0 + operand * (1.0 - squash))


def ring_order(n):
    down = 4 if n % 8 == 0 else 1
    across = n // down
    order = [i * across for i in range(down)]
    for back, i in enumerate(reversed(range(down))):
        row = range(1, across) if back % 2 == 0 else reversed(range(1, across))
        order += [i * across + j for j in row]
    return order


class Ring:
    def __init__(self):
        self.n = lax.axis_size("chan")
        self.order = ring_order(self.n)
        self.table = jnp.array(self.order, jnp.int32)
        place = [0] * self.n
        for k, i in enumerate(self.order):
            place[i] = k
        self.place = jnp.array(place, jnp.int32)[lax.axis_index("chan")]
        self.right = [(self.order[k], self.order[(k + 1) % self.n]) for k in range(self.n)]
        self.left = [(b, a) for a, b in self.right]

    def owner(self, away):
        return self.table[(self.place + away + self.n) % self.n]

    def go_right(self, x):
        return lax.ppermute(x, "chan", self.right)

    def go_left(self, x):
        return lax.ppermute(x, "chan", self.left)

    def blocks(self, x):
        half = self.n // 2
        cut = x.shape[0] // 2
        from_left, from_right = x, x
        found = [(self.owner(0), x)]
        for step in range(1, half):
            from_left, from_right = self.go_right(from_left), self.go_left(from_right)
            found += [(self.owner(-step), from_left), (self.owner(step), from_right)]
        far = jnp.concatenate([self.go_right(from_left[:cut]), self.go_left(from_right[cut:])], axis=0)
        return found + [(self.owner(half), far)]

    def gather(self, x):
        rows = x.shape[0]
        whole = jnp.zeros((self.n * rows,) + x.shape[1:], x.dtype)
        for owner, block in self.blocks(x):
            whole = lax.dynamic_update_slice_in_dim(whole, block, owner * rows, 0)
        return whole

    def scatter(self, part):
        half = self.n // 2
        rows = part.shape[0] // self.n
        cut = rows // 2
        mine = lambda away: lax.dynamic_slice_in_dim(part, self.owner(away) * rows, rows, 0)
        wide = lambda v: v.astype(f32)
        far = mine(half).astype(bf16)
        right, left = self.go_right(far[:cut]), self.go_left(far[cut:])
        for away in range(half - 1, 0, -1):
            ahead, behind = wide(mine(away)), wide(mine(-away))
            if away == half - 1:
                ahead = jnp.concatenate([ahead[:cut] + wide(right), ahead[cut:]], axis=0)
                behind = jnp.concatenate([behind[:cut], behind[cut:] + wide(left)], axis=0)
            else:
                ahead, behind = ahead + wide(right), behind + wide(left)
            right, left = self.go_right(ahead.astype(bf16)), self.go_left(behind.astype(bf16))
        return wide(mine(0)) + wide(right) + wide(left)


def is_power(n):
    return n & (n - 1) == 0


def bits_of(n):
    return [1 << b for b in range(n.bit_length() - 1)]


def sum_chan(x, wire):
    n = lax.axis_size("chan")
    index = lax.axis_index("chan")
    if not is_power(n) or x.shape[0] % (16 * n):
        return lax.psum(x, "chan")
    perm = lambda b: [(i, i ^ b) for i in range(n)]
    for b in bits_of(n):
        h = x.shape[0] // 2
        upper = (index // b) % 2
        keep = lax.dynamic_slice_in_dim(x, upper * h, h, 0)
        send = lax.dynamic_slice_in_dim(x, (1 - upper) * h, h, 0)
        x = keep + lax.ppermute(send.astype(wire), "chan", perm(b)).astype(f32)
    x = x.astype(wire)
    for b in reversed(bits_of(n)):
        upper = (index // b) % 2
        other = lax.ppermute(x, "chan", perm(b))
        x = jnp.concatenate([jnp.where(upper == 0, x, other), jnp.where(upper == 0, other, x)], axis=0)
    return x


def small_gather(x, axis):
    n = lax.axis_size(axis)
    if not is_power(n) or n > 8:
        return lax.all_gather(x, axis, axis=0)
    index = lax.axis_index(axis)
    every = jnp.stack([x] + [lax.ppermute(x, axis, [(i, i ^ k) for i in range(n)]) for k in range(1, n)])
    return unmix(every, index, n)


def unmix(every, index, n):
    shape = every.shape
    levels = bits_of(n)
    every = every.reshape((2,) * len(levels) + shape[1:])
    for place, b in enumerate(reversed(levels)):
        every = jnp.where((index // b) % 2 == 1, jnp.flip(every, place), every)
    return every.reshape(shape)


def small_scatter(x):
    n = lax.axis_size("chan")
    if not is_power(n) or n > 8:
        return lax.psum_scatter(x, "chan", scatter_dimension=0, tiled=False)
    mixed = unmix(x, lax.axis_index("chan"), n)
    return sum([lax.ppermute(mixed[k], "chan", [(i, i ^ k) for i in range(n)]) for k in range(1, n)], mixed[0])


def sum_rows(x, wire):
    n = lax.axis_size("rows")
    if n != 4:
        return lax.psum(x, "rows")
    core = [(0, 1), (1, 0), (2, 3), (3, 2)]
    chip = [(0, 2), (2, 0), (1, 3), (3, 1)]
    upper = lax.axis_index("rows") % 2
    h = x.shape[0] // 2
    keep = lax.dynamic_slice_in_dim(x, upper * h, h, 0)
    send = lax.dynamic_slice_in_dim(x, (1 - upper) * h, h, 0)
    pair = (keep + lax.ppermute(send, "rows", core)).astype(wire)
    total = pair.astype(f32) + lax.ppermute(pair, "rows", chip).astype(f32)
    other = lax.ppermute(total, "rows", core)
    return jnp.concatenate([jnp.where(upper == 0, total, other), jnp.where(upper == 0, other, total)], axis=0)


def local(
    activations,
    condition,
    seq_lengths,
    w_ada,
    b_ada,
    norm_gain,
    w_in_x,
    w_in_z,
    conv_weight,
    conv_bias,
    w_xproj,
    w_dt,
    dt_bias,
    a_log,
    d_skip,
    w_out,
    grad_out,
):
    ring = Ring()
    tok_loc, width = activations.shape
    low_rank = w_dt.shape[0]
    states = a_log.shape[1]
    channels = a_log.shape[0]
    conv_taps = conv_weight.shape[1]
    parts = lax.axis_size("chan")
    tok_count = tok_loc * parts
    tok_start = lax.axis_index("chan") * tok_loc
    seq_lens = seq_lengths[0]
    seq_count = seq_lens.shape[0]
    seq_ends = jnp.cumsum(seq_lens)
    begins = seq_ends - seq_lens
    position = jnp.arange(tok_count, dtype=jnp.int32)
    member = (position[:, None] >= begins[None, :]) & (position[:, None] < seq_ends[None, :])
    onehot = member.astype(f32)
    in_seq = jnp.sum(onehot * (position[:, None] - begins[None, :]).astype(f32), axis=1)
    per_token = lambda rows, hot: sum(hot[:, s : s + 1] * rows[s][None] for s in range(seq_count))
    cond_act = jax.nn.silu(condition.astype(f32)).astype(bf16)
    cond_all = small_gather(cond_act, "rows").reshape(-1, width)
    modulation = (
        jnp.einsum("si,kji->skj", cond_act, w_ada, preferred_element_type=f32) + b_ada[None]
    )
    part_width = norm_gain.shape[0]
    packed = jnp.concatenate([modulation.reshape(3 * seq_count, part_width), norm_gain[None]], axis=0)
    packed = small_gather(packed, "chan").transpose(1, 0, 2).reshape(3 * seq_count + 1, width)
    mod_full = packed[: 3 * seq_count].reshape(seq_count, 3, width)
    gain_full = packed[3 * seq_count]
    whole = ring.gather(activations)
    whole_up = ring.gather(grad_out)
    shift_tok = per_token(mod_full[:, 0], onehot)
    scale_tok = per_token(mod_full[:, 1], onehot)
    gate_tok = per_token(mod_full[:, 2], onehot)
    wide = whole.astype(f32)
    centred = wide - jnp.mean(wide, axis=1, keepdims=True)
    inv_std = lax.rsqrt(jnp.mean(centred * centred, axis=1, keepdims=True) + EPSILON)
    normed = centred * inv_std
    xmod = (normed * gain_full[None] * (1.0 + scale_tok) + shift_tok).astype(bf16)
    x_inner = dot_across(xmod, w_in_x)
    conv_pre = jnp.zeros_like(x_inner) + conv_bias[None, :]
    for tap_index in range(conv_taps):
        lag = conv_taps - 1 - tap_index
        valid = (in_seq >= lag).astype(f32)[:, None]
        conv_pre = conv_pre + conv_weight[:, tap_index][None, :] * delay_rows(x_inner, lag) * valid
    act_low = jax.nn.silu(conv_pre).astype(bf16)
    act = act_low.astype(f32)
    proj = sum_chan(low_dot(act_low, w_xproj), PROJ_WIRE)
    dt_low = proj[:, :low_rank].astype(bf16)
    b_mat = proj[:, low_rank : low_rank + states].astype(f32)
    c_mat = proj[:, low_rank + states :].astype(f32)
    dt_raw = low_dot(dt_low, w_dt) + dt_bias[None, :]
    deltas = jax.nn.softplus(dt_raw)
    a_neg = -jnp.exp(a_log).T
    z_inner = dot_across(xmod, w_in_z)
    gate_z = jax.nn.silu(z_inner)
    d_branch_all = (whole_up.astype(f32) * gate_tok).astype(bf16)
    d_gated = dot_across(d_branch_all, w_out)
    d_mixed = d_gated * gate_z
    y, d_deltas, d_act_scan, d_log, d_b_part, d_c_part = scans(
        deltas, act_low, d_mixed, a_neg, b_mat, c_mat, begins[None]
    )
    d_dt_raw = d_deltas * jax.nn.sigmoid(dt_raw)
    d_dt_low = d_dt_raw.astype(bf16)
    proj_terms = jnp.concatenate([dot_across(d_dt_low, w_dt), d_b_part, d_c_part], axis=1)
    d_proj = sum_chan(proj_terms, DPROJ_WIRE).astype(bf16)
    mixed = y + d_skip[None, :] * act
    gated = (mixed * gate_z).astype(bf16)
    branch_part = low_dot(gated, w_out).astype(bf16)
    branch = ring.scatter(branch_part)
    onehot_loc = lax.dynamic_slice_in_dim(onehot, tok_start, tok_loc, 0)
    block_out = (activations.astype(f32) + per_token(mod_full[:, 2], onehot_loc) * branch).astype(bf16)
    grad_w_out = sum_rows(dot_tokens(gated, d_branch_all), bf16)
    d_z_low = (d_gated * mixed * silu_slope(z_inner)).astype(bf16)
    grad_w_in_z = sum_rows(dot_tokens(d_z_low, xmod), bf16)
    d_act = d_mixed * d_skip[None, :] + d_act_scan + dot_across(d_proj, w_xproj)
    d_conv = d_act * silu_slope(conv_pre)
    d_x_inner = jnp.zeros_like(d_conv)
    tap_grads = []
    for tap_index in range(conv_taps):
        lag = conv_taps - 1 - tap_index
        valid = (in_seq >= lag).astype(f32)[:, None]
        masked = d_conv * valid
        tap_grads.append(jnp.sum(masked * delay_rows(x_inner, lag), axis=0))
        d_x_inner = d_x_inner + conv_weight[:, tap_index][None, :] * advance_rows(masked, lag)
    d_x_low = d_x_inner.astype(bf16)
    d_xmod_part = (low_dot(d_x_low, w_in_x) + low_dot(d_z_low, w_in_z)).astype(bf16)
    d_xmod = ring.scatter(d_xmod_part)
    grad_w_in_x = sum_rows(dot_tokens(d_x_low, xmod), bf16)
    small = jnp.concatenate(
        [
            dot_tokens(d_proj, act_low),
            dot_tokens(dt_low, d_dt_low),
            d_log * a_neg,
            jnp.stack(tap_grads),
            jnp.sum(d_conv, axis=0)[None],
            jnp.sum(d_dt_raw, axis=0)[None],
            jnp.sum(d_mixed * act, axis=0)[None],
        ],
        axis=0,
    )
    small = jnp.pad(small, ((0, -small.shape[0] % 16), (0, 0)))
    small = sum_rows(small, f32)
    counts = [w_xproj.shape[1], low_rank, states, conv_taps, 1, 1, 1]
    pieces, at = [], 0
    for count in counts:
        pieces.append(small[at : at + count])
        at += count
    share = d_xmod_part.astype(f32)
    share_normed = share * normed
    share_gate = whole_up.astype(f32) * branch_part.astype(f32)
    seq_sum = lambda v: jnp.stack([jnp.sum(onehot[:, s : s + 1] * v, axis=0) for s in range(seq_count)])
    sums = jnp.stack([seq_sum(share), seq_sum(share_normed), seq_sum(share_gate)], axis=1)
    sums = small_scatter(sums.reshape(seq_count, 3, parts, part_width).transpose(2, 0, 1, 3))
    gain_term = jnp.sum(sums[:, 1] * (1.0 + modulation[:, 1]), axis=0)
    d_mod = jnp.stack([sums[:, 0], sums[:, 1] * norm_gain[None], sums[:, 2]], axis=1)
    reach = jnp.concatenate([d_mod.reshape(3 * seq_count, part_width), gain_term[None]], axis=0)
    reach = small_gather(reach, "rows")
    grad_gain = jnp.sum(reach[:, 3 * seq_count], axis=0)
    d_mod_all = reach[:, : 3 * seq_count].reshape(-1, 3, part_width)
    grad_b_ada = jnp.sum(d_mod_all, axis=0)
    grad_w_ada = jnp.einsum(
        "skj,si->kji",
        d_mod_all,
        cond_all.astype(f32),
        precision=HIGHEST,
        preferred_element_type=f32,
    )
    wide_loc = activations.astype(f32)
    centred_loc = wide_loc - jnp.mean(wide_loc, axis=1, keepdims=True)
    inv_std_loc = lax.rsqrt(jnp.mean(centred_loc * centred_loc, axis=1, keepdims=True) + EPSILON)
    normed_loc = centred_loc * inv_std_loc
    scale_loc = per_token(mod_full[:, 1], onehot_loc)
    d_normed = d_xmod * (1.0 + scale_loc) * gain_full[None, :]
    mean_first = jnp.mean(d_normed, axis=1, keepdims=True)
    mean_second = jnp.mean(d_normed * normed_loc, axis=1, keepdims=True)
    grad_input = (
        inv_std_loc * (d_normed - mean_first - normed_loc * mean_second) + grad_out.astype(f32)
    ).astype(bf16)
    return (
        block_out,
        grad_input,
        grad_w_ada,
        grad_b_ada,
        grad_gain,
        grad_w_in_x,
        grad_w_in_z,
        pieces[3].T,
        pieces[4][0],
        pieces[0].T,
        pieces[1],
        pieces[5][0],
        pieces[2].T,
        pieces[6][0],
        grad_w_out,
    )


PROJ_WIRE = bf16
DPROJ_WIRE = bf16


def solution(mesh):
    return jax.shard_map(
        local,
        mesh=mesh,
        in_specs=(
            P(("rows", "chan"), None),
            P("rows", None),
            P("rows", None),
            P(None, "chan", None),
            P(None, "chan"),
            P("chan"),
            P("chan", None),
            P("chan", None),
            P("chan", None),
            P("chan"),
            P("chan", None),
            P(None, "chan"),
            P("chan"),
            P("chan", None),
            P("chan"),
            P("chan", None),
            P(("rows", "chan"), None),
        ),
        out_specs=(
            P(("rows", "chan"), None),
            P(("rows", "chan"), None),
            P(None, "chan", None),
            P(None, "chan"),
            P("chan"),
            P("chan", None),
            P("chan", None),
            P("chan", None),
            P("chan"),
            P("chan", None),
            P(None, "chan"),
            P("chan"),
            P("chan", None),
            P("chan"),
            P("chan", None),
        ),
        check_vma=False,
    )
```

profile of v0, /device:TPU:0, one launch (start us, length us, event | category | flops | bytes accessed | tf_op | source)
XLA Modules:
  0.0 561.2 jit_solution(12900246771661514676)
XLA Ops:
  72.2 4.8 collective-permute-done.23
  79.1 8.5 %collective-permute-done.9 = bf16[160,1536]{1,0:T(8,128)(2,1)S(1)} collective-permute-done((bf16[160,1536]{1,0:T(8,128)(2,1)S(1)}, bf16[160,1536]{1,0:T(8,128)(2,1)S(1)}, u32[]{:S(2)}, u32[]{:S(2)}) %collective-permute-start.9) | collective-permute-done | bytes 491552 | tf_op jit(solution)/shard_map/ppermute | solution.py:234
  92.9 15.3 %collective-permute-done.11 = bf16[160,1536]{1,0:T(8,128)(2,1)S(1)} collective-permute-done((bf16[160,1536]{1,0:T(8,128)(2,1)S(1)}, bf16[160,1536]{1,0:T(8,128)(2,1)S(1)}, u32[]{:S(2)}, u32[]{:S(2)}) %collective-permute-start.11) | collective-permute-done | bytes 491552 | tf_op jit(solution)/shard_map/ppermute | solution.py:234
  115.3 3.8 collective-permute-done.13
  130.6 8.0 %fusion.5 = (bf16[1280,1536]{1,0:T(8,128)(2,1)S(1)}, bf16[1280,1536]{1,0:T(8,128)(2,1)S(1)}) fusion(bf16[1280,1536]{1,0:T(8,128)(2,1)} %maximum_dynamic-update-slice_fusion, f32[1536]{0:T(1024)S(1)} %get-tuple-element.86, f32[1536]{0:T(1024)S(1)} %get-tuple-element.87, f32[1536]{0:T(1024)S(1)} %get-tuple-element.88, f32[1280]{0:T(1024)S(1)} %get-tuple-element.94, ...), kind=kLoop, calls=%fused_computation.13 | loop fusion | flops 39321600 | bytes 15792128 | tf_op jit(solution)/shard_map/convert_element_type | solution.py:402
  143.4 6.2 %fusion.13 = (f32[384]{0:T(512)}, f32[1280,384]{1,0:T(8,128)}, bf16[1280,384]{1,0:T(8,128)(2,1)S(1)}, f32[1280,384]{1,0:T(8,128)}, f32[1280,384]{1,0:T(8,128)}) fusion(f32[1280,384]{1,0:T(8,128)S(1)} %fusion.71, f32[1280]{0:T(1024)S(1)} %get-tuple-element.174, f32[1280,384]{1,0:T(8,128)S(1)} %fusion.69, f32[384]{0:T(512)S(1)} %copy-done.94, ...), kind=kOutput, calls=%fused_computation.34 | convolution fusion | flops 1522237056 | bytes 21843968 | tf_op jit(solution)/shard_map/dot_general | solution.py:182
  152.9 4.3 collective-permute-done.15
  182.0 4.6 collective-permute-done.20
  203.9 135.9 %scan_all.1 = (f32[1280,384]{1,0:T(8,128)}, f32[1280,384]{1,0:T(8,128)}, f32[1280,384]{1,0:T(8,128)}, f32[16,384]{1,0:T(8,128)}, f32[80,256]{1,0:T(8,128)}, /*index=5*/f32[80,256]{1,0:T(8,128)}) custom-call(s32[1,2]{1,0:T(1,128)} %copy-done.109, f32[1280,384]{1,0:T(8,128)} %get-tuple-element.190.delta_ref, bf16[1280,384]{1,0:T(8,128)(2,1)} %copy-done.3, ...), custom_call_target="tpu_custom_call" | custom-call | flops 471859200 | bytes 11796480 | tf_op jit(solution)/shard_map/scan_all/pallas_call | solution.py:154
  346.7 4.1 convolution_convert_fusion
  361.7 4.3 fusion.74
  378.1 5.6 collective-permute-done.39
  384.1 5.0 collective-permute-done.40
  390.1 3.7 collective-permute-done.41
  395.7 3.8 collective-permute-done.42
  411.4 9.5 %multiply_reduce_fusion.3 = (f32[1536]{0:T(1024)S(1)}, f32[1536]{0:T(1024)S(1)}, f32[1536]{0:T(1024)S(1)}, f32[1536]{0:T(1024)S(1)}, f32[1536]{0:T(1024)S(1)}, /*index=5*/f32[1536]{0:T(1024)S(1)}, bf16[1280,1536]{1,0:T(8,128)(2,1)}) fusion(bf16[1280,1536]{1,0:T(8,128)(2,1)} %maximum_dynamic-update-slice_fusion, f32[1280]{0:T(1024)S(1)} %copy-done.76, ...), kind=kOutput, calls=%fused_computation.21 | convolution fusion | flops 1553193984 | bytes 25812992 | tf_op jit(solution)/shard_map/dot_general | solution.py:178
  449.6 7.6 %collective-permute-done.30 = bf16[160,1536]{1,0:T(8,128)(2,1)S(1)} collective-permute-done((bf16[160,1536]{1,0:T(8,128)(2,1)}, bf16[160,1536]{1,0:T(8,128)(2,1)S(1)}, u32[]{:S(2)}, u32[]{:S(2)}) %collective-permute-start.30) | collective-permute-done | bytes 491552 | tf_op jit(solution)/shard_map/ppermute | solution.py:234
  461.9 4.4 collective-permute-done.47
  468.0 4.0 collective-permute-done.71
  480.9 7.0 %collective-permute-done.31 = bf16[160,1536]{1,0:T(8,128)(2,1)} collective-permute-done((bf16[160,1536]{1,0:T(8,128)(2,1)}, bf16[160,1536]{1,0:T(8,128)(2,1)}, u32[]{:S(2)}, u32[]{:S(2)}) %collective-permute-start.31) | collective-permute-done | bytes 491552 | tf_op jit(solution)/shard_map/ppermute | solution.py:234
  491.3 6.2 %collective-permute-done.44 = bf16[160,1536]{1,0:T(8,128)(2,1)S(1)} collective-permute-done((bf16[160,1536]{1,0:T(8,128)(2,1)}, bf16[160,1536]{1,0:T(8,128)(2,1)S(1)}, u32[]{:S(2)}, u32[]{:S(2)}) %collective-permute-start.44) | collective-permute-done | bytes 491552 | tf_op jit(solution)/shard_map/ppermute | solution.py:234
  508.7 13.7 %collective-permute-done.45 = bf16[160,1536]{1,0:T(8,128)(2,1)S(1)} collective-permute-done((bf16[160,1536]{1,0:T(8,128)(2,1)S(1)}, bf16[160,1536]{1,0:T(8,128)(2,1)S(1)}, u32[]{:S(2)}, u32[]{:S(2)}) %collective-permute-start.45) | collective-permute-done | bytes 491552 | tf_op jit(solution)/shard_map/ppermute | solution.py:234
  524.0 12.4 %collective-permute-done.49 = bf16[160,1536]{1,0:T(8,128)(2,1)S(1)} collective-permute-done((bf16[160,1536]{1,0:T(8,128)(2,1)S(1)}, bf16[160,1536]{1,0:T(8,128)(2,1)S(1)}, u32[]{:S(2)}, u32[]{:S(2)}) %collective-permute-start.49) | collective-permute-done | bytes 491552 | tf_op jit(solution)/shard_map/ppermute | solution.py:237
  539.4 9.9 %collective-permute-done.46 = bf16[160,1536]{1,0:T(8,128)(2,1)S(1)} collective-permute-done((bf16[160,1536]{1,0:T(8,128)(2,1)S(1)}, bf16[160,1536]{1,0:T(8,128)(2,1)S(1)}, u32[]{:S(2)}, u32[]{:S(2)}) %collective-permute-start.46) | collective-permute-done | bytes 491552 | tf_op jit(solution)/shard_map/ppermute | solution.py:234
  (570 shorter events, 254.9 us)
Async XLA Ops:
  0.7 62.0 %collective-permute-start.21 = (bf16[160,1536]{1,0:T(8,128)(2,1)}, bf16[160,1536]{1,0:T(8,128)(2,1)}, u32[]{:S(2)}, u32[]{:S(2)}) collective-permute-start(bf16[160,1536]{1,0:T(8,128)(2,1)} %param.35), channel_id=1, source_target_pairs={{0,2},{2,4},{4,6},{6,7},{7,5},{5,3},{3,1},{1,0},{8,10},{10,12},{12... | collective-permute-start | bytes 1474568 | tf_op jit(solution)/shard_map/ppermute | solution.py:234
  3.8 59.0 %collective-permute-start.22 = (bf16[160,1536]{1,0:T(8,128)(2,1)}, bf16[160,1536]{1,0:T(8,128)(2,1)}, u32[]{:S(2)}, u32[]{:S(2)}) collective-permute-start(bf16[160,1536]{1,0:T(8,128)(2,1)} %param.35), channel_id=1, source_target_pairs={{2,0},{4,2},{6,4},{7,6},{5,7},{3,5},{1,3},{0,1},{10,8},{12,10},{14... | collective-permute-start | bytes 1474568 | tf_op jit(solution)/shard_map/ppermute | solution.py:237
  3.8 61.0 %collective-permute-start.7 = (bf16[160,1536]{1,0:T(8,128)(2,1)}, bf16[160,1536]{1,0:T(8,128)(2,1)S(1)}, u32[]{:S(2)}, u32[]{:S(2)}) collective-permute-start(bf16[160,1536]{1,0:T(8,128)(2,1)} %param.19), channel_id=1, source_target_pairs={{0,2},{2,4},{4,6},{6,7},{7,5},{5,3},{3,1},{1,0},{8,10},{10,12},{12... | collective-permute-start | bytes 1474568 | tf_op jit(solution)/shard_map/ppermute | solution.py:234
  5.8 59.1 %collective-permute-start.8 = (bf16[160,1536]{1,0:T(8,128)(2,1)}, bf16[160,1536]{1,0:T(8,128)(2,1)S(1)}, u32[]{:S(2)}, u32[]{:S(2)}) collective-permute-start(bf16[160,1536]{1,0:T(8,128)(2,1)} %param.19), channel_id=1, source_target_pairs={{2,0},{4,2},{6,4},{7,6},{5,7},{3,5},{1,3},{0,1},{10,8},{12,10},{14... | collective-permute-start | bytes 1474568 | tf_op jit(solution)/shard_map/ppermute | solution.py:237
  7.8 24.4 %collective-permute-start = (f32[7,192]{1,0:T(8,128)S(1)}, f32[7,192]{1,0:T(8,128)S(1)}, u32[]{:S(2)}, u32[]{:S(2)}) collective-permute-start(f32[7,192]{1,0:T(8,128)S(1)} %get-tuple-element.113), channel_id=1, source_target_pairs={{0,1},{1,0},{2,3},{3,2},{4,5},{5,4},{6,7},{7,6},{8,9},{9,8},{10,11... | collective-permute-start | bytes 16136 | tf_op jit(solution)/shard_map/ppermute | solution.py:309
  62.3 110.9 %collective-permute-start.61 = (bf16[2,1536]{1,0:T(2,128)(2,1)}, bf16[2,1536]{1,0:T(2,128)(2,1)}, u32[]{:S(2)}, u32[]{:S(2)}) collective-permute-start(bf16[2,1536]{1,0:T(2,128)(2,1)} %fusion.43), channel_id=1, source_target_pairs={{0,8},{8,0},{16,24},{24,16},{1,9},{9,1},{17,25},{25,17},{2,10},{10... | collective-permute-start | bytes 18440 | tf_op jit(solution)/shard_map/ppermute | solution.py:309
  64.8 22.7 %collective-permute-start.9 = (bf16[160,1536]{1,0:T(8,128)(2,1)S(1)}, bf16[160,1536]{1,0:T(8,128)(2,1)S(1)}, u32[]{:S(2)}, u32[]{:S(2)}) collective-permute-start(bf16[160,1536]{1,0:T(8,128)(2,1)S(1)} %collective-permute-done.7), channel_id=1, source_target_pairs={{0,2},{2,4},{4,6},{6,7},{7,5},{5,3},{3,1},{1,0},{8,10},{10,12},{12... | collective-permute-start | bytes 1474568 | tf_op jit(solution)/shard_map/ppermute | solution.py:234
  64.9 22.7 %collective-permute-start.10 = (bf16[160,1536]{1,0:T(8,128)(2,1)S(1)}, bf16[160,1536]{1,0:T(8,128)(2,1)S(1)}, u32[]{:S(2)}, u32[]{:S(2)}) collective-permute-start(bf16[160,1536]{1,0:T(8,128)(2,1)S(1)} %collective-permute-done.8), channel_id=1, source_target_pairs={{2,0},{4,2},{6,4},{7,6},{5,7},{3,5},{1,3},{0,1},{10,8},{12,10},{14... | collective-permute-start | bytes 1474568 | tf_op jit(solution)/shard_map/ppermute | solution.py:237
  77.0 33.8 %collective-permute-start.25 = (bf16[160,1536]{1,0:T(8,128)(2,1)S(1)}, bf16[160,1536]{1,0:T(8,128)(2,1)S(1)}, u32[]{:S(2)}, u32[]{:S(2)}) collective-permute-start(bf16[160,1536]{1,0:T(8,128)(2,1)S(1)} %collective-permute-done.23), channel_id=1, source_target_pairs={{0,2},{2,4},{4,6},{6,7},{7,5},{5,3},{3,1},{1,0},{8,10},{10,12},{12... | collective-permute-start | bytes 1474568 | tf_op jit(solution)/shard_map/ppermute | solution.py:234
  77.1 36.4 %collective-permute-start.26 = (bf16[160,1536]{1,0:T(8,128)(2,1)S(1)}, bf16[160,1536]{1,0:T(8,128)(2,1)S(1)}, u32[]{:S(2)}, u32[]{:S(2)}) collective-permute-start(bf16[160,1536]{1,0:T(8,128)(2,1)S(1)} %collective-permute-done.24), channel_id=1, source_target_pairs={{2,0},{4,2},{6,4},{7,6},{5,7},{3,5},{1,3},{0,1},{10,8},{12,10},{14... | collective-permute-start | bytes 1474568 | tf_op jit(solution)/shard_map/ppermute | solution.py:237
  87.5 20.7 %collective-permute-start.11 = (bf16[160,1536]{1,0:T(8,128)(2,1)S(1)}, bf16[160,1536]{1,0:T(8,128)(2,1)S(1)}, u32[]{:S(2)}, u32[]{:S(2)}) collective-permute-start(bf16[160,1536]{1,0:T(8,128)(2,1)S(1)} %collective-permute-done.9), channel_id=1, source_target_pairs={{0,2},{2,4},{4,6},{6,7},{7,5},{5,3},{3,1},{1,0},{8,10},{10,12},{12... | collective-permute-start | bytes 1474568 | tf_op jit(solution)/shard_map/ppermute | solution.py:234
  87.6 22.2 %collective-permute-start.12 = (bf16[160,1536]{1,0:T(8,128)(2,1)S(1)}, bf16[160,1536]{1,0:T(8,128)(2,1)S(1)}, u32[]{:S(2)}, u32[]{:S(2)}) collective-permute-start(bf16[160,1536]{1,0:T(8,128)(2,1)S(1)} %collective-permute-done.10), channel_id=1, source_target_pairs={{2,0},{4,2},{6,4},{7,6},{5,7},{3,5},{1,3},{0,1},{10,8},{12,10},{14... | collective-permute-start | bytes 1474568 | tf_op jit(solution)/shard_map/ppermute | solution.py:237
  108.2 65.0 %collective-permute-start.62 = (bf16[2,1536]{1,0:T(2,128)(2,1)}, bf16[2,1536]{1,0:T(2,128)(2,1)}, u32[]{:S(2)}, u32[]{:S(2)}) collective-permute-start(bf16[2,1536]{1,0:T(2,128)(2,1)} %fusion.43), channel_id=1, source_target_pairs={{0,16},{8,24},{16,0},{24,8},{1,17},{9,25},{17,1},{25,9},{2,18},{10... | collective-permute-start | bytes 18440 | tf_op jit(solution)/shard_map/ppermute | solution.py:309
  109.8 63.4 %collective-permute-start.63 = (bf16[2,1536]{1,0:T(2,128)(2,1)}, bf16[2,1536]{1,0:T(2,128)(2,1)}, u32[]{:S(2)}, u32[]{:S(2)}) collective-permute-start(bf16[2,1536]{1,0:T(2,128)(2,1)} %fusion.43), channel_id=1, source_target_pairs={{0,24},{8,16},{16,8},{24,0},{1,25},{9,17},{17,9},{25,1},{2,26},{10... | collective-permute-start | bytes 18440 | tf_op jit(solution)/shard_map/ppermute | solution.py:309
  436.4 40.4 %collective-permute-start.73 = (f32[192,1536]{1,0:T(8,128)}, f32[192,1536]{1,0:T(8,128)}, u32[]{:S(2)}, u32[]{:S(2)}) collective-permute-start(f32[192,1536]{1,0:T(8,128)} %constant_dynamic-slice_fusion.5), channel_id=1, source_target_pairs={{0,8},{8,0},{16,24},{24,16},{1,9},{9,1},{17,25},{25,17},{2,10},{10... | collective-permute-start | bytes 3538952 | tf_op jit(solution)/shard_map/ppermute | solution.py:340
  436.4 53.6 %collective-permute-start.67 = (f32[192,1536]{1,0:T(8,128)}, f32[192,1536]{1,0:T(8,128)S(1)}, u32[]{:S(2)}, u32[]{:S(2)}) collective-permute-start(f32[192,1536]{1,0:T(8,128)} %constant_dynamic-slice_fusion.6), channel_id=1, source_target_pairs={{0,8},{8,0},{16,24},{24,16},{1,9},{9,1},{17,25},{25,17},{2,10},{10... | collective-permute-start | bytes 3538952 | tf_op jit(solution)/shard_map/ppermute | solution.py:340
  459.2 21.6 %collective-permute-start.34 = (bf16[160,1536]{1,0:T(8,128)(2,1)S(1)}, bf16[160,1536]{1,0:T(8,128)(2,1)}, u32[]{:S(2)}, u32[]{:S(2)}) collective-permute-start(bf16[160,1536]{1,0:T(8,128)(2,1)S(1)} %copy-done.46), channel_id=1, source_target_pairs={{2,0},{4,2},{6,4},{7,6},{5,7},{3,5},{1,3},{0,1},{10,8},{12,10},{14... | collective-permute-start | bytes 1474568 | tf_op jit(solution)/shard_map/ppermute | solution.py:237
  461.9 41.4 %collective-permute-start.64 = (f32[192,1536]{1,0:T(8,128)}, f32[192,1536]{1,0:T(8,128)}, u32[]{:S(2)}, u32[]{:S(2)}) collective-permute-start(f32[192,1536]{1,0:T(8,128)} %constant_dynamic-slice_fusion.7), channel_id=1, source_target_pairs={{0,8},{8,0},{16,24},{24,16},{1,9},{9,1},{17,25},{25,17},{2,10},{10... | collective-permute-start | bytes 3538952 | tf_op jit(solution)/shard_map/ppermute | solution.py:340
  476.9 30.1 %collective-permute-start.48 = (bf16[160,1536]{1,0:T(8,128)(2,1)S(1)}, bf16[160,1536]{1,0:T(8,128)(2,1)S(1)}, u32[]{:S(2)}, u32[]{:S(2)}) collective-permute-start(bf16[160,1536]{1,0:T(8,128)(2,1)S(1)} %pad_maximum_fusion.7), channel_id=1, source_target_pairs={{2,0},{4,2},{6,4},{7,6},{5,7},{3,5},{1,3},{0,1},{10,8},{12,10},{14... | collective-permute-start | bytes 1474568 | tf_op jit(solution)/shard_map/ppermute | solution.py:237
  497.5 25.2 %collective-permute-start.68 = (bf16[192,1536]{1,0:T(8,128)(2,1)S(1)}, bf16[192,1536]{1,0:T(8,128)(2,1)S(1)}, u32[]{:S(2)}, u32[]{:S(2)}) collective-permute-start(bf16[192,1536]{1,0:T(8,128)(2,1)S(1)} %add_convert_fusion.2), channel_id=1, source_target_pairs={{0,16},{16,0},{8,24},{24,8},{1,17},{17,1},{9,25},{25,9},{2,18},{18... | collective-permute-start | bytes 1769480 | tf_op jit(solution)/shard_map/ppermute | solution.py:341
  501.5 37.3 %collective-permute-start.32 = (bf16[160,1536]{1,0:T(8,128)(2,1)S(1)}, bf16[160,1536]{1,0:T(8,128)(2,1)S(1)}, u32[]{:S(2)}, u32[]{:S(2)}) collective-permute-start(bf16[160,1536]{1,0:T(8,128)(2,1)S(1)} %get-tuple-element.124), channel_id=1, source_target_pairs={{0,2},{2,4},{4,6},{6,7},{7,5},{5,3},{3,1},{1,0},{8,10},{10,12},{12... | collective-permute-start | bytes 1474568 | tf_op jit(solution)/shard_map/ppermute | solution.py:234
  505.5 33.4 %collective-permute-start.36 = (bf16[160,1536]{1,0:T(8,128)(2,1)S(1)}, bf16[160,1536]{1,0:T(8,128)(2,1)S(1)}, u32[]{:S(2)}, u32[]{:S(2)}) collective-permute-start(bf16[160,1536]{1,0:T(8,128)(2,1)S(1)} %add_convert_fusion.8), channel_id=1, source_target_pairs={{2,0},{4,2},{6,4},{7,6},{5,7},{3,5},{1,3},{0,1},{10,8},{12,10},{14... | collective-permute-start | bytes 1474568 | tf_op jit(solution)/shard_map/ppermute | solution.py:237
  507.0 30.8 %collective-permute-start.65 = (bf16[192,1536]{1,0:T(8,128)(2,1)S(1)}, bf16[192,1536]{1,0:T(8,128)(2,1)S(1)}, u32[]{:S(2)}, u32[]{:S(2)}) collective-permute-start(bf16[192,1536]{1,0:T(8,128)(2,1)S(1)} %add_convert_fusion.3), channel_id=1, source_target_pairs={{0,16},{16,0},{8,24},{24,8},{1,17},{17,1},{9,25},{25,9},{2,18},{18... | collective-permute-start | bytes 1769480 | tf_op jit(solution)/shard_map/ppermute | solution.py:341
  522.4 32.1 %collective-permute-start.75 = (f32[192,1536]{1,0:T(8,128)S(1)}, f32[192,1536]{1,0:T(8,128)S(1)}, u32[]{:S(2)}, u32[]{:S(2)}) collective-permute-start(f32[192,1536]{1,0:T(8,128)S(1)} %convert_add_fusion.1), channel_id=1, source_target_pairs={{0,8},{8,0},{16,24},{24,16},{1,9},{9,1},{17,25},{25,17},{2,10},{10... | collective-permute-start | bytes 3538952 | tf_op jit(solution)/shard_map/ppermute | solution.py:342
  (171 other events, 3052.5 us)
where the time goes:
time: 568 us; the launch traced here: 561 us
  waiting for transfers between devices  161 us (28%)
  Pallas kernels  136 us (24%)
  starting transfers between devices  80.6 us (14%)
  other arithmetic  61.1 us (11%)
  local copies, waits for them, and re-layouts  59.9 us (11%)
  matrix products  49.1 us (9%)
  between operations  13.6 us (2%)
    pallas_call x1, Pallas kernels, scans(): pl.pallas_call(functools.partial(scan_kernel, begins.shape[1], row_mode),...  136 us
    ppermute x16, waiting for transfers between devices, go_right(): return lax.ppermute(x, 'chan', self.right)  78.6 us
    ppermute x16, waiting for transfers between devices, go_left(): return lax.ppermute(x, 'chan', self.left)  22.8 us
    ppermute x6, waiting for transfers between devices, sum_chan(): other = lax.ppermute(x, 'chan', perm(b))  21.4 us
    ppermute x13, starting transfers between devices, small_gather(): lax.ppermute(x, axis, [(i, i ^ k) for i in range(n)])  21.3 us
    dot_general x5, matrix products, low_dot(): return jnp.dot(left, right, preferred_element_type=f32)  19.5 us
    ppermute x13, waiting for transfers between devices, small_gather(): lax.ppermute(x, axis, [(i, i ^ k) for i in range(n)])  16.1 us
    ppermute x16, starting transfers between devices, go_left(): return lax.ppermute(x, 'chan', self.left)  15.9 us
  transfers between devices with their start and end apart: 76, of which 37 were waited for; matrix products, arithmetic and copies ran while one was open for 18% of the time, Pallas kernels for 0%

commit v1 on v0

v1 whole, which is shorter than its diff:
```python
import functools
import math

import jax
import jax.numpy as jnp
from jax import lax
from jax.experimental import pallas as pl
from jax.experimental.pallas import tpu as pltpu
from jax.sharding import PartitionSpec as P

CHUNK = 16
LANES = 128
LOG2E = math.log2(math.e)
f32 = jnp.float32
bf16 = jnp.bfloat16


def scan_kernel(
    n_seq,
    states,
    begins_ref,
    proj_ref,
    act_ref,
    z_ref,
    d_gated_ref,
    w_dt_ref,
    dt_bias_ref,
    an_ref,
    skip_ref,
    gated_ref,
    d_z_ref,
    d_dt_ref,
    d_act_ref,
    ga_ref,
    sums_ref,
    terms_ref,
    b_all,
    c_all,
    pf_all,
    db_all,
    b_blk_all,
    c_blk_all,
    delta_all,
    step_all,
    dm_all,
    exp_all,
):
    tokens, channels = act_ref.shape
    n_pairs = tokens // (2 * CHUNK)
    wide = CHUNK * states
    low_rank = proj_ref.shape[1] - 2 * states
    an = an_ref[...]
    a2 = an * LOG2E
    dot = functools.partial(jnp.dot, preferred_element_type=f32)
    across = functools.partial(
        lax.dot_general, dimension_numbers=(((1,), (1,)), ((), ())), preferred_element_type=f32
    )

    def diagonal(rows):
        r = lax.broadcasted_iota(jnp.int32, (rows, wide), 0) % CHUNK
        return (r == lax.broadcasted_iota(jnp.int32, (rows, wide), 1) // states).astype(f32)

    diag = diagonal(CHUNK)
    ones_blk = diag.astype(bf16)
    m = lax.broadcasted_iota(jnp.int32, (low_rank + 2 * states, wide), 0)
    q = lax.broadcasted_iota(jnp.int32, (low_rank + 2 * states, wide), 1) % states
    pick_b = (m == low_rank + q).astype(bf16)
    pick_c = (m == low_rank + states + q).astype(bf16)
    tile = pl.program_id(0)

    @pl.when(tile == 0)
    def _():
        many = diagonal(LANES)

        def spread(k, carry):
            base = pl.multiple_of(k * LANES, LANES)
            proj = proj_ref[pl.ds(base, LANES), :]
            low = proj.astype(bf16)
            b_blk_all[pl.ds(base, LANES), :] = (dot(low, pick_b) * many).astype(bf16)
            c_blk_all[pl.ds(base, LANES), :] = (dot(low, pick_c) * many).astype(bf16)
            turned = proj.astype(f32).T
            bt = turned[low_rank : low_rank + states]
            ct = turned[low_rank + states :]
            for i in range(LANES):
                at = pl.ds(pl.multiple_of(base * states + i * states, states), states)
                b_all[at, :] = jnp.broadcast_to(bt[:, i : i + 1], (states, channels))
                c_all[at, :] = jnp.broadcast_to(ct[:, i : i + 1], (states, channels))
            return carry

        lax.fori_loop(0, tokens // LANES, spread, 0)

    def prepare(k, carry):
        here = pl.ds(pl.multiple_of(k * LANES, LANES), LANES)
        dt_raw = dot(proj_ref[here, :].astype(bf16), w_dt_ref[...]) + dt_bias_ref[...]
        delta = jnp.maximum(dt_raw, 0.0) + jnp.log1p(jnp.exp(-jnp.abs(dt_raw)))
        delta_all[here, :] = delta
        step_all[here, :] = delta * act_ref[here, :].astype(f32)
        z = z_ref[here, :]
        dm_all[here, :] = d_gated_ref[here, :] * (z * jax.nn.sigmoid(z))
        return carry

    lax.fori_loop(0, tokens // LANES, prepare, 0)

    def keep_at(t):
        keep = None
        for s in range(1, n_seq):
            k = jnp.where(begins_ref[0, s] == t, 0.0, 1.0).astype(f32)
            keep = k if keep is None else keep * k
        return keep

    def sweep(body, cut, carry):
        plain, masked = functools.partial(body, False), functools.partial(body, True)
        if n_seq == 1:
            return lax.fori_loop(0, n_pairs, plain, carry)
        if n_seq > 2:
            return lax.fori_loop(0, n_pairs, masked, carry)
        carry = lax.fori_loop(0, cut, plain, carry)
        carry = masked(cut, carry)
        return lax.fori_loop(cut + 1, n_pairs, plain, carry)

    def row(ref, t):
        return ref[pl.ds(t, 1), :]

    def forward(masked, pair, carry):
        sf, g = carry
        base = pl.multiple_of(pair * 2 * CHUNK, 2 * CHUNK)
        for i in range(2 * CHUNK):
            at = pl.ds(pl.multiple_of(base * states + i * states, states), states)
            decay = jnp.exp2(row(delta_all, base + i) * a2)
            if masked:
                keep = keep_at(base + i)
                sf = sf * keep
                g = g * keep
            pf = decay * sf
            sf = pf + row(step_all, base + i) * b_all[at, :]
            db = row(dm_all, base + i) * c_all[at, :] + g
            g = decay * db
            pf_all[at, :] = pf
            db_all[at, :] = db
        return sf, g

    zero = jnp.zeros((states, channels), f32)
    first = begins_ref[0, n_seq - 1]
    sweep(forward, first // (2 * CHUNK), (zero, zero))

    def backward(masked, k, carry):
        sb, g, ga = carry
        base = pl.multiple_of((n_pairs - 1 - k) * 2 * CHUNK, 2 * CHUNK)
        for i in range(2 * CHUNK - 1, -1, -1):
            at = pl.ds(pl.multiple_of(base * states + i * states, states), states)
            delta = row(delta_all, base + i)
            decay = jnp.exp2(delta * a2)
            drive = row(step_all, base + i) * b_all[at, :]
            if masked:
                keep = keep_at(base + i + 1)
                sb = sb * keep
                g = g * keep
            pb = decay * sb
            sb = pb + drive
            df = row(dm_all, base + i) * c_all[at, :] + g
            g = decay * df
            pf = pf_all[at, :]
            db = db_all[at, :]
            d_expo = df * pf + db * pb
            ga = ga + d_expo * delta
            pf_all[at, :] = pf + drive + sb
            db_all[at, :] = df + db
            exp_all[at, :] = (d_expo * an).astype(bf16)
        return sb, g, ga

    cut = n_pairs - 1 - (first - 1) // (2 * CHUNK)
    _, _, ga = sweep(backward, cut, (zero, zero, zero))
    ga_ref[...] = ga

    def finish(k, carry):
        by_bias, by_skip = carry
        base = pl.multiple_of(k * LANES, LANES)
        here = pl.ds(base, LANES)
        low = proj_ref[here, :].astype(bf16)
        act = act_ref[here, :].astype(f32)
        d_mixed = dm_all[here, :]
        dm_low = d_mixed.astype(bf16)
        step_low = step_all[here, :].astype(bf16)
        y, through, expo, dcm, dbm = [], [], [], [], []
        for c in range(LANES // CHUNK):
            at = pl.ds(pl.multiple_of(base * states + c * wide, wide), wide)
            mine = pl.ds(pl.multiple_of(base + c * CHUNK, CHUNK), CHUNK)
            span = slice(c * CHUNK, (c + 1) * CHUNK)
            both = pf_all[at, :].astype(bf16)
            drv = db_all[at, :].astype(bf16)
            y.append(dot(c_blk_all[mine, :], both))
            through.append(dot(b_blk_all[mine, :], drv))
            expo.append(dot(ones_blk, exp_all[at, :]))
            dcm.append((across(dm_low[span], both) * diag).astype(bf16))
            dbm.append((across(step_low[span], drv) * diag).astype(bf16))
        whole = lambda parts: jnp.concatenate(parts, axis=0)
        skip = skip_ref[...]
        z = z_ref[here, :]
        sigma = jax.nn.sigmoid(z)
        mixed = whole(y) + skip * act
        gated_ref[here, :] = (mixed * (z * sigma)).astype(bf16)
        d_z_ref[here, :] = (d_gated_ref[here, :] * mixed * (sigma * (1.0 + z * (1.0 - sigma)))).astype(bf16)
        via = whole(through)
        d_act_ref[here, :] = d_mixed * skip + via * delta_all[here, :]
        dt_raw = dot(low, w_dt_ref[...]) + dt_bias_ref[...]
        d_dt_raw = (whole(expo) + via * act) * jax.nn.sigmoid(dt_raw)
        d_dt = d_dt_raw.astype(bf16)
        d_dt_ref[here, :] = d_dt
        terms = across(d_dt, w_dt_ref[...]) + across(whole(dbm), pick_b) + across(whole(dcm), pick_c)

        @pl.when(tile == 0)
        def _():
            terms_ref[here, :] = terms

        @pl.when(tile != 0)
        def _():
            terms_ref[here, :] += terms

        total = lambda v: jnp.sum(v, axis=0, keepdims=True)
        return by_bias + total(d_dt_raw), by_skip + total(d_mixed * act)

    none = jnp.zeros((1, channels), f32)
    by_bias, by_skip = lax.fori_loop(0, tokens // LANES, finish, (none, none))
    sums_ref[0:8, :] = jnp.broadcast_to(by_bias, (8, channels))
    sums_ref[8:16, :] = jnp.broadcast_to(by_skip, (8, channels))


def scans(proj, act_low, z_inner, d_gated, w_dt, dt_bias, a_neg, d_skip, begins):
    tokens, channels = act_low.shape
    states = a_neg.shape[0]
    tile = LANES if channels % LANES == 0 else channels
    wide = CHUNK * states
    w_dt = jnp.pad(w_dt, ((0, 2 * states), (0, 0)))
    col = lambda: pl.BlockSpec((tokens, tile), lambda j: (0, j))
    rows = lambda n: pl.BlockSpec((n, tile), lambda j: (0, j))
    full = lambda: pl.BlockSpec(proj.shape, lambda j: (0, 0))
    sds = jax.ShapeDtypeStruct
    return pl.pallas_call(
        functools.partial(scan_kernel, begins.shape[1], states),
        grid=(channels // tile,),
        in_specs=[
            pl.BlockSpec(memory_space=pltpu.SMEM),
            full(),
            col(),
            col(),
            col(),
            rows(w_dt.shape[0]),
            rows(1),
            rows(states),
            rows(1),
        ],
        out_specs=[col(), col(), col(), col(), rows(states), rows(16), full()],
        out_shape=[
            sds((tokens, channels), bf16),
            sds((tokens, channels), bf16),
            sds((tokens, channels), bf16),
            sds((tokens, channels), f32),
            sds((states, channels), f32),
            sds((16, channels), f32),
            sds(proj.shape, f32),
        ],
        scratch_shapes=[pltpu.VMEM((tokens * states, tile), f32)] * 4
        + [pltpu.VMEM((tokens, wide), bf16)] * 2
        + [pltpu.VMEM((tokens, tile), f32)] * 3
        + [pltpu.VMEM((tokens * states, tile), bf16)],
        compiler_params=pltpu.CompilerParams(vmem_limit_bytes=62 * 2**20, dimension_semantics=("arbitrary",)),
        cost_estimate=pl.CostEstimate(
            flops=tokens * channels * states * 60,
            bytes_accessed=tokens * channels * 24,
            transcendentals=2 * tokens * channels * states,
        ),
        name="scan_all",
    )(begins, proj, act_low, z_inner, d_gated, w_dt, dt_bias[None], a_neg, d_skip[None])


EPSILON = 1e-06
HIGHEST = lax.Precision.HIGHEST


def low_dot(left, right):
    return jnp.dot(left, right, preferred_element_type=f32)


def dot_across(left, right):
    return lax.dot_general(left, right, (((1,), (1,)), ((), ())), preferred_element_type=f32)


def dot_tokens(left, right):
    return lax.dot_general(left, right, (((0,), (0,)), ((), ())), preferred_element_type=f32)


def delay_rows(operand, lag):
    if lag == 0:
        return operand
    padding = jnp.zeros((lag,) + operand.shape[1:], operand.dtype)
    return jnp.concatenate([padding, operand[:-lag]], axis=0)


def advance_rows(operand, lag):
    if lag == 0:
        return operand
    padding = jnp.zeros((lag,) + operand.shape[1:], operand.dtype)
    return jnp.concatenate([operand[lag:], padding], axis=0)


def after(x, *others):
    return lax.optimization_barrier((x,) + others)[0]


def silu_slope(operand):
    squash = jax.nn.sigmoid(operand)
    return squash * (1.0 + operand * (1.0 - squash))


class Ring:
    def __init__(self):
        self.n = lax.axis_size("chan")
        self.down = 4 if self.n % 8 == 0 else 1
        self.across = self.n // self.down
        order = [self.at(p) for p in range(self.n)]
        self.right = [(order[k], order[(k + 1) % self.n]) for k in range(self.n)]
        self.left = [(b, a) for a, b in self.right]
        index = lax.axis_index("chan")
        i, j = index // self.across, index % self.across
        back = self.down - 1 - i
        step = jnp.where(back % 2 == 0, j - 1, self.across - 1 - j)
        self.place = jnp.where(j == 0, i, self.down + back * (self.across - 1) + step)

    def at(self, p):
        if self.down == 1:
            return p
        back, step = (p - self.down) // (self.across - 1), (p - self.down) % (self.across - 1)
        if isinstance(p, int):
            column = 1 + step if back % 2 == 0 else self.across - 1 - step
            return p * self.across if p < self.down else (self.down - 1 - back) * self.across + column
        column = jnp.where(back % 2 == 0, 1 + step, self.across - 1 - step)
        return jnp.where(p < self.down, p * self.across, (self.down - 1 - back) * self.across + column)

    def owner(self, away):
        p = self.place + away
        if away > 0:
            p = jnp.where(p >= self.n, p - self.n, p)
        elif away < 0:
            p = jnp.where(p < 0, p + self.n, p)
        return self.at(p)

    def go_right(self, x):
        return lax.ppermute(x, "chan", self.right)

    def go_left(self, x):
        return lax.ppermute(x, "chan", self.left)

    def blocks(self, x):
        half = self.n // 2
        cut = x.shape[0] // 2
        from_left, from_right = x, x
        found = [(self.owner(0), x)]
        for step in range(1, half):
            from_left, from_right = self.go_right(from_left), self.go_left(from_right)
            found += [(self.owner(-step), from_left), (self.owner(step), from_right)]
        far = jnp.concatenate([self.go_right(from_left[:cut]), self.go_left(from_right[cut:])], axis=0)
        return found + [(self.owner(half), far)]

    def whole(self, blocks, *others):
        rows = blocks[0][1].shape[0]
        whole = jnp.zeros((self.n * rows,) + blocks[0][1].shape[1:], blocks[0][1].dtype)
        if others:
            whole = after(whole, *others)
        for owner, block in blocks:
            whole = lax.dynamic_update_slice_in_dim(whole, block, owner * rows, 0)
        return whole

    def scatter(self, part, stages=None):
        half = self.n // 2
        rows = part.shape[0] // self.n
        cut = rows // 2
        mine = lambda away: lax.dynamic_slice_in_dim(part, self.owner(away) * rows, rows, 0)
        wide = lambda v: v.astype(f32)
        far = mine(half)
        right, left = self.go_right(far[:cut]), self.go_left(far[cut:])
        sent, arrived = [(far,)], [(right, left)]
        for away in range(half - 1, 0, -1):
            ahead, behind = wide(mine(away)), wide(mine(-away))
            if away == half - 1:
                ahead = jnp.concatenate([ahead[:cut] + wide(right), ahead[cut:]], axis=0)
                behind = jnp.concatenate([behind[:cut], behind[cut:] + wide(left)], axis=0)
            else:
                ahead, behind = ahead + wide(right), behind + wide(left)
            ahead, behind = ahead.astype(bf16), behind.astype(bf16)
            held = (stages or {}).get(half - away)
            if held:
                ahead, behind = lax.optimization_barrier((ahead, behind) + tuple(held))[:2]
            sent.append((ahead, behind))
            right, left = self.go_right(ahead), self.go_left(behind)
            arrived.append((right, left))
        return wide(mine(0)) + wide(right) + wide(left), arrived, sent


def is_power(n):
    return n & (n - 1) == 0


def bits_of(n):
    return [1 << b for b in range(n.bit_length() - 1)]


def sum_chan(x, wire, stages=None):
    n = lax.axis_size("chan")
    index = lax.axis_index("chan")
    if not is_power(n) or x.shape[0] % (16 * n):
        x = lax.psum(x, "chan")
        return x, [x] * 8
    perm = lambda b: [(i, i ^ b) for i in range(n)]
    arrived = []

    def exchange(send, b):
        held = (stages or {}).get(len(arrived))
        if held:
            send = after(send, *held)
        arrived.append(lax.ppermute(send, "chan", perm(b)))
        return arrived[-1]

    for b in bits_of(n):
        h = x.shape[0] // 2
        upper = (index // b) % 2
        keep = lax.dynamic_slice_in_dim(x, upper * h, h, 0)
        send = lax.dynamic_slice_in_dim(x, (1 - upper) * h, h, 0)
        x = keep + exchange(send.astype(wire), b).astype(f32)
    x = x.astype(wire)
    for b in reversed(bits_of(n)):
        upper = (index // b) % 2
        other = exchange(x, b)
        x = jnp.concatenate([jnp.where(upper == 0, x, other), jnp.where(upper == 0, other, x)], axis=0)
    return x, arrived


def small_gather(x, axis, stages=()):
    n = lax.axis_size(axis)
    if not is_power(n) or n > 8:
        return lax.all_gather(x, axis, axis=0)
    index = lax.axis_index(axis)
    x = x[None]
    for level, b in enumerate(bits_of(n)):
        if level < len(stages):
            x = after(x, *stages[level])
        other = lax.ppermute(x, axis, [(i, i ^ b) for i in range(n)])
        lower = (index // b) % 2 == 0
        x = jnp.concatenate([jnp.where(lower, x, other), jnp.where(lower, other, x)], axis=0)
    return x


def small_sum(x, stages):
    n = lax.axis_size("chan")
    if not is_power(n) or n > 8:
        return lax.psum(x, "chan")
    for level, b in enumerate(bits_of(n)):
        other = lax.ppermute(x, "chan", [(i, i ^ b) for i in range(n)])
        x, other = lax.optimization_barrier((x, other) + tuple(stages[level]))[:2]
        x = x + other
    return x


def sum_rows(x, wire, stages=((), ())):
    n = lax.axis_size("rows")
    if n != 4:
        return lax.psum(x, "rows")
    other = lax.ppermute(x, "rows", [(0, 1), (1, 0), (2, 3), (3, 2)])
    x, other = lax.optimization_barrier((x, other) + tuple(stages[0]))[:2]
    pair = (x + other).astype(wire)
    other = lax.ppermute(pair, "rows", [(0, 2), (2, 0), (1, 3), (3, 1)])
    pair, other = lax.optimization_barrier((pair, other) + tuple(stages[1]))[:2]
    return pair.astype(f32) + other.astype(f32)


def place_norm_kernel(n_seq, count, owners_ref, begins_ref, mod_ref, *refs):
    blocks, (xmod_ref, normed_ref, held) = refs[:count], refs[count:]
    rows, width = xmod_ref.shape
    step = 2 * CHUNK if rows % (2 * CHUNK) == 0 else rows
    k = pl.program_id(0)
    base = owners_ref[k] * rows

    def hold(block_ref):
        held[...] = block_ref[...]

    for i in range(count):
        pl.when(k == i)(functools.partial(hold, blocks[i]))
    shift, scale = mod_ref[0:1, :], mod_ref[1:2, :]
    gain = mod_ref[3 * n_seq : 3 * n_seq + 1, :]
    for start in range(0, rows, step):
        here = slice(start, start + step)
        wide = held[here, :].astype(f32)
        centred = wide - jnp.sum(wide, axis=1, keepdims=True) * (1.0 / width)
        square = jnp.sum(centred * centred, axis=1, keepdims=True) * (1.0 / width)
        normed = centred * lax.rsqrt(square + EPSILON)
        token = base + start + lax.broadcasted_iota(jnp.int32, (step, 1), 0)
        add, by = shift, gain * (1.0 + scale)
        for s in range(1, n_seq):
            later = token >= begins_ref[0, s]
            add = jnp.where(later, mod_ref[3 * s : 3 * s + 1, :], add)
            by = jnp.where(later, gain * (1.0 + mod_ref[3 * s + 1 : 3 * s + 2, :]), by)
        xmod_ref[here, :] = (normed * by + add).astype(bf16)
        normed_ref[here, :] = normed.astype(bf16)


def place_gate_kernel(n_seq, count, owners_ref, begins_ref, mod_ref, *refs):
    blocks, (gated_ref, plain_ref) = refs[:count], refs[count:]
    rows = gated_ref.shape[0]
    step = CHUNK if rows % CHUNK == 0 else rows
    k = pl.program_id(0)
    base = owners_ref[k] * rows

    def fill(block_ref):
        def part(p, carry):
            here = pl.ds(pl.multiple_of(p * step, step), step)
            low = block_ref[here, :]
            token = base + p * step + lax.broadcasted_iota(jnp.int32, (step, 1), 0)
            gate = mod_ref[2:3, :]
            for s in range(1, n_seq):
                gate = jnp.where(token >= begins_ref[0, s], mod_ref[3 * s + 2 : 3 * s + 3, :], gate)
            gated_ref[here, :] = (low.astype(f32) * gate).astype(bf16)
            plain_ref[here, :] = low
            return carry

        lax.fori_loop(0, rows // step, part, 0)

    for i in range(count):
        pl.when(k == i)(functools.partial(fill, blocks[i]))


def place(kernel, blocks, begins, mod, name, scratch=False):
    owners = jnp.stack([owner for owner, _ in blocks]).astype(jnp.int32)
    parts = [block for _, block in blocks]
    rows, width = parts[0].shape
    count = len(parts)
    whole = jax.ShapeDtypeStruct((count * rows, width), bf16)
    out = lambda: pl.BlockSpec((rows, width), lambda k, owners_ref, begins_ref: (owners_ref[k], 0))
    fixed = lambda shape: pl.BlockSpec(shape, lambda k, owners_ref, begins_ref: (0, 0))
    return pl.pallas_call(
        functools.partial(kernel, begins.shape[1], count),
        grid_spec=pltpu.PrefetchScalarGridSpec(
            num_scalar_prefetch=2,
            grid=(count,),
            in_specs=[fixed(mod.shape)] + [fixed((rows, width))] * count,
            out_specs=[out(), out()],
            scratch_shapes=[pltpu.VMEM((rows, width), bf16)] if scratch else [],
        ),
        out_shape=[whole, whole],
        compiler_params=pltpu.CompilerParams(vmem_limit_bytes=28 * 2**20, dimension_semantics=("arbitrary",)),
        cost_estimate=pl.CostEstimate(
            flops=count * rows * width * 20, bytes_accessed=count * rows * width * 6, transcendentals=0
        ),
        name=name,
    )(owners, begins, mod, *parts)


def sums_kernel(n_seq, begins_ref, share_ref, normed_ref, up_ref, branch_ref, out_ref):
    rows, width = share_ref.shape
    k = pl.program_id(0)

    @pl.when(k == 0)
    def _():
        out_ref[...] = jnp.zeros(out_ref.shape, f32)

    lanes = 2 * LANES if width % (2 * LANES) == 0 else width
    token = k * rows + lax.broadcasted_iota(jnp.int32, (rows, 1), 0)
    for at in range(0, width, lanes):
        cols = slice(at, at + lanes)
        share = share_ref[:, cols].astype(f32)
        terms = [share, share * normed_ref[:, cols].astype(f32)]
        terms.append(up_ref[:, cols].astype(f32) * branch_ref[:, cols].astype(f32))
        for j, term in enumerate(terms):
            rest = jnp.sum(term, axis=0, keepdims=True)
            for s in range(n_seq - 1, 0, -1):
                later = jnp.sum(jnp.where(token >= begins_ref[0, s], term, 0.0), axis=0, keepdims=True)
                at_row = j * n_seq + s
                mine = later if s == n_seq - 1 else later - after_it
                out_ref[at_row : at_row + 1, cols] += mine
                after_it = later
            out_ref[j * n_seq : j * n_seq + 1, cols] += rest - (after_it if n_seq > 1 else 0.0)


def token_sums(share, normed, up, branch, begins):
    tokens, width = share.shape
    n_seq = begins.shape[1]
    rows = LANES
    spec = lambda: pl.BlockSpec((rows, width), lambda k: (k, 0))
    height = 3 * n_seq + (-3 * n_seq % 8)
    return pl.pallas_call(
        functools.partial(sums_kernel, n_seq),
        grid=(tokens // rows,),
        in_specs=[pl.BlockSpec(memory_space=pltpu.SMEM), spec(), spec(), spec(), spec()],
        out_specs=pl.BlockSpec((height, width), lambda k: (0, 0)),
        out_shape=jax.ShapeDtypeStruct((height, width), f32),
        compiler_params=pltpu.CompilerParams(vmem_limit_bytes=32 * 2**20, dimension_semantics=("arbitrary",)),
        cost_estimate=pl.CostEstimate(flops=tokens * width * 12, bytes_accessed=tokens * width * 8, transcendentals=0),
        name="token_sums",
    )(begins, share, normed, up, branch)


def local(
    activations,
    condition,
    seq_lengths,
    w_ada,
    b_ada,
    norm_gain,
    w_in_x,
    w_in_z,
    conv_weight,
    conv_bias,
    w_xproj,
    w_dt,
    dt_bias,
    a_log,
    d_skip,
    w_out,
    grad_out,
):
    ring = Ring()
    tok_loc, width = activations.shape
    low_rank = w_dt.shape[0]
    states = a_log.shape[1]
    channels = a_log.shape[0]
    conv_taps = conv_weight.shape[1]
    tok_count = tok_loc * ring.n
    tok_start = lax.axis_index("chan") * tok_loc
    act_blocks = ring.blocks(activations)
    act_in = [b for _, b in act_blocks[1:]]
    cond_act = jax.nn.silu(condition.astype(f32)).astype(bf16)
    modulation = (
        jnp.einsum("si,kji->skj", cond_act, w_ada, preferred_element_type=f32) + b_ada[None]
    )
    part_width = norm_gain.shape[0]
    seq_count = seq_lengths.shape[1]
    packed = jnp.concatenate([modulation.reshape(3 * seq_count, part_width), norm_gain[None]], axis=0)
    packed = small_gather(packed, "chan", [(), act_in[0:2], act_in[2:4]])
    seq_lengths, conv_weight, conv_bias, w_dt, dt_bias, a_log, d_skip = lax.optimization_barrier(
        (seq_lengths, conv_weight, conv_bias, w_dt, dt_bias, a_log, d_skip, act_in[2], act_in[3])
    )[:7]
    seq_lens = seq_lengths[0]
    seq_ends = jnp.cumsum(seq_lens)
    begins = seq_ends - seq_lens
    position = jnp.arange(tok_count, dtype=jnp.int32)
    member = (position[:, None] >= begins[None, :]) & (position[:, None] < seq_ends[None, :])
    onehot = member.astype(f32)
    in_seq = jnp.sum(onehot * (position[:, None] - begins[None, :]).astype(f32), axis=1)
    per_token = lambda rows, hot: sum(hot[:, s : s + 1] * rows[s][None] for s in range(seq_count))
    packed = packed.transpose(1, 0, 2).reshape(3 * seq_count + 1, width)
    packed = jnp.pad(packed, ((0, -packed.shape[0] % 8), (0, 0)))
    mod_full = packed[: 3 * seq_count].reshape(seq_count, 3, width)
    gain_full = packed[3 * seq_count]
    a_neg = -jnp.exp(a_log).T
    up_blocks = ring.blocks(after(grad_out, act_in[-1]))
    up_in = [b for _, b in up_blocks[1:]]
    xmod, normed = place(place_norm_kernel, act_blocks, begins[None], packed, "place_norm", True)
    x_inner = dot_across(after(xmod, *up_in[0:2]), w_in_x)
    conv_pre = jnp.zeros_like(x_inner) + conv_bias[None, :]
    for tap_index in range(conv_taps):
        lag = conv_taps - 1 - tap_index
        valid = (in_seq >= lag).astype(f32)[:, None]
        conv_pre = conv_pre + conv_weight[:, tap_index][None, :] * delay_rows(x_inner, lag) * valid
    act_low = jax.nn.silu(conv_pre).astype(bf16)
    proj, proj_in = sum_chan(low_dot(act_low, w_xproj), PROJ_WIRE, {1: up_in[2:4], 3: up_in[4:6]})
    dt_low = proj[:, :low_rank].astype(bf16)
    z_inner = dot_across(after(xmod, act_low), w_in_z)
    d_branch_all, whole_up = place(place_gate_kernel, up_blocks, begins[None], packed, "place_gate")
    d_gated = dot_across(d_branch_all, w_out)
    gated, d_z_low, d_dt_low, d_act, d_log, bias_skip, proj_terms = scans(
        proj, act_low, z_inner, d_gated, w_dt, dt_bias, a_neg, d_skip, begins[None]
    )
    branch_part = lax.optimization_barrier(low_dot(gated, w_out).astype(bf16))
    branch, branch_in, branch_out = ring.scatter(branch_part)
    d_proj, d_proj_in = sum_chan(proj_terms, DPROJ_WIRE, {2: branch_in[0], 5: branch_in[1]})
    d_proj = d_proj.astype(bf16)
    onehot_loc = lax.dynamic_slice_in_dim(onehot, tok_start, tok_loc, 0)
    block_out = (activations.astype(f32) + per_token(mod_full[:, 2], onehot_loc) * branch).astype(bf16)
    gated, d_z_grad = lax.optimization_barrier((gated, d_z_low) + branch_out[0])[:2]
    grad_w_out = sum_rows(dot_tokens(gated, d_branch_all), bf16, (d_proj_in[1:2], branch_in[-1]))
    grad_w_in_z = sum_rows(dot_tokens(d_z_grad, xmod), bf16, (d_proj_in[2:3], branch_in[-1]))
    d_act = d_act + dot_across(d_proj, w_xproj)
    d_conv = d_act * silu_slope(conv_pre)
    d_x_inner = jnp.zeros_like(d_conv)
    tap_grads = []
    for tap_index in range(conv_taps):
        lag = conv_taps - 1 - tap_index
        valid = (in_seq >= lag).astype(f32)[:, None]
        masked = d_conv * valid
        tap_grads.append(jnp.sum(masked * delay_rows(x_inner, lag), axis=0))
        d_x_inner = d_x_inner + conv_weight[:, tap_index][None, :] * advance_rows(masked, lag)
    d_x_low = d_x_inner.astype(bf16)
    d_xmod_part = (low_dot(d_x_low, w_in_x) + low_dot(d_z_low, w_in_z)).astype(bf16)
    d_xmod_part = after(d_xmod_part, *branch_in[-1])
    d_xmod, d_xmod_in, d_xmod_out = ring.scatter(d_xmod_part, {2: (grad_w_out, grad_w_in_z), 3: (block_out,)})
    ins = (d_xmod_in + [d_xmod_in[-1]] * 4)[:4]
    outs = (d_xmod_out + [d_xmod_out[-1]] * 4)[:4]
    d_x_grad = after(d_x_low, *outs[0])
    d_proj, d_xmod_share = lax.optimization_barrier((d_proj, d_xmod_part) + outs[1])[:2]
    grad_w_in_x = sum_rows(dot_tokens(d_x_grad, xmod), bf16, (ins[0], ins[2]))
    small = jnp.concatenate(
        [
            dot_tokens(d_proj, act_low),
            dot_tokens(dt_low, d_dt_low),
            d_log * a_neg,
            jnp.stack(tap_grads),
            jnp.sum(d_conv, axis=0)[None],
            bias_skip[0:1],
            bias_skip[8:9],
        ],
        axis=0,
    )
    small = jnp.pad(small, ((0, -small.shape[0] % 16), (0, 0)))
    small = sum_rows(small, f32, (ins[1], ins[2]))
    counts = [w_xproj.shape[1], low_rank, states, conv_taps, 1, 1, 1]
    pieces, at = [], 0
    for count in counts:
        pieces.append(small[at : at + count])
        at += count
    sums = token_sums(d_xmod_share, normed, whole_up, branch_part, begins[None])
    sums = small_sum(sums, (ins[1], ins[2], ins[3]))
    sums = lax.dynamic_slice_in_dim(sums, lax.axis_index("chan") * part_width, part_width, 1)
    by_shift, by_scale, by_gate = [sums[k * seq_count : (k + 1) * seq_count] for k in range(3)]
    gain_term = jnp.sum(by_scale * (1.0 + modulation[:, 1]), axis=0)
    d_mod = jnp.stack([by_shift, by_scale * norm_gain[None], by_gate], axis=1)
    reach = jnp.concatenate([d_mod.reshape(3 * seq_count, part_width), gain_term[None]], axis=0)
    reach = small_gather(reach, "rows")
    cond_all = small_gather(after(cond_act, act_in[-1]), "rows").reshape(-1, width)
    grad_gain = jnp.sum(reach[:, 3 * seq_count], axis=0)
    d_mod_all = reach[:, : 3 * seq_count].reshape(-1, 3, part_width)
    grad_b_ada = jnp.sum(d_mod_all, axis=0)
    grad_w_ada = jnp.einsum(
        "skj,si->kji",
        d_mod_all,
        cond_all.astype(f32),
        precision=HIGHEST,
        preferred_element_type=f32,
    )
    wide_loc = activations.astype(f32)
    centred_loc = wide_loc - jnp.mean(wide_loc, axis=1, keepdims=True)
    inv_std_loc = lax.rsqrt(jnp.mean(centred_loc * centred_loc, axis=1, keepdims=True) + EPSILON)
    normed_loc = centred_loc * inv_std_loc
    scale_loc = per_token(mod_full[:, 1], onehot_loc)
    d_normed = d_xmod * (1.0 + scale_loc) * gain_full[None, :]
    mean_first = jnp.mean(d_normed, axis=1, keepdims=True)
    mean_second = jnp.mean(d_normed * normed_loc, axis=1, keepdims=True)
    grad_input = (
        inv_std_loc * (d_normed - mean_first - normed_loc * mean_second) + grad_out.astype(f32)
    ).astype(bf16)
    return (
        block_out,
        grad_input,
        grad_w_ada,
        grad_b_ada,
        grad_gain,
        grad_w_in_x,
        grad_w_in_z,
        pieces[3].T,
        pieces[4][0],
        pieces[0].T,
        pieces[1],
        pieces[5][0],
        pieces[2].T,
        pieces[6][0],
        grad_w_out,
    )


PROJ_WIRE = bf16
DPROJ_WIRE = bf16


def solution(mesh):
    return jax.shard_map(
        local,
        mesh=mesh,
        in_specs=(
            P(("rows", "chan"), None),
            P("rows", None),
            P("rows", None),
            P(None, "chan", None),
            P(None, "chan"),
            P("chan"),
            P("chan", None),
            P("chan", None),
            P("chan", None),
            P("chan"),
            P("chan", None),
            P(None, "chan"),
            P("chan"),
            P("chan", None),
            P("chan"),
            P("chan", None),
            P(("rows", "chan"), None),
        ),
        out_specs=(
            P(("rows", "chan"), None),
            P(("rows", "chan"), None),
            P(None, "chan", None),
            P(None, "chan"),
            P("chan"),
            P("chan", None),
            P("chan", None),
            P("chan", None),
            P("chan"),
            P("chan", None),
            P(None, "chan"),
            P("chan"),
            P("chan", None),
            P("chan"),
            P("chan", None),
        ),
        check_vma=False,
    )
```

time: 568 us -> 394 us (0.69)
  Pallas kernels: 136 us -> 90.1 us
  waiting for transfers between devices: 161 us -> 124 us
  local copies, waits for them, and re-layouts: 59.9 us -> 27.3 us
  other arithmetic: 61.1 us -> 39.9 us
  matrix products: 49.1 us -> 32.7 us
  between operations: 13.6 us -> 2.42 us
  starting transfers between devices: 80.6 us -> 69.7 us
    pallas_call x1 -> x4, Pallas kernels: 136 us -> 90.1 us  [the longest x1 74.8 us: scans(): pl.pallas_call(functools.partial(scan_kernel, begins.shape[1], states), g...]
    ppermute x16, waiting for transfers between devices: 78.6 us -> 35.3 us  [go_right(): return lax.ppermute(x, 'chan', self.right)]
    ppermute x44 -> x30, starting transfers between devices: 51.3 us -> 35.8 us  [the longest x12 15.1 us: exchange(): arrived.append(lax.ppermute(send, 'chan', perm(b)))]
    dynamic_update_slice x14 -> x0, local copies, waits for them, and re-layouts: 13.6 us -> none  [gather(): whole = lax.dynamic_update_slice_in_dim(whole, block, owner * rows, 0)]
    unnamed x245 -> x130, local copies, waits for them, and re-layouts: 8.25 us -> 20.3 us
    another operation x15 -> x2, local copies, waits for them, and re-layouts: 11.9 us -> 0.09 us  [the longest x1 0.08 us: place(): owners = jnp.stack([owner for owner, _ in blocks]).astype(jnp.int32)]
    dot_general x5 -> x4, matrix products: 19.5 us -> 8.42 us  [low_dot(): return jnp.dot(left, right, preferred_element_type=f32)]
    convert_element_type x13 -> x10, other arithmetic: 22.8 us -> 13.3 us  [the longest x3 5.88 us: sum_rows(): pair = (x + other).astype(wire)]
  transfers between devices with their start and end apart: 76 -> 62, of which waited for: 37 -> 35; matrix products, arithmetic and copies ran while one was open for 18% -> 16% of each run, Pallas kernels for 0% -> 4%
where the time goes in v1:
time: 394 us; the launch traced here: 386 us
  waiting for transfers between devices  124 us (31%)
  Pallas kernels  90.1 us (23%)
  starting transfers between devices  69.7 us (18%)
  other arithmetic  39.9 us (10%)
  matrix products  32.7 us (8%)
  local copies, waits for them, and re-layouts  27.3 us (7%)
    pallas_call x1, Pallas kernels, scans(): pl.pallas_call(functools.partial(scan_kernel, begins.shape[1], states), g...  74.8 us
    ppermute x16, waiting for transfers between devices, go_right(): return lax.ppermute(x, 'chan', self.right)  35.3 us
    ppermute x12, waiting for transfers between devices, exchange(): arrived.append(lax.ppermute(send, 'chan', perm(b)))  26.6 us
    ppermute x16, waiting for transfers between devices, go_left(): return lax.ppermute(x, 'chan', self.left)  25.2 us
    unnamed x130, local copies, waits for them, and re-layouts  20.3 us
    ppermute x4, waiting for transfers between devices, sum_rows(): other = lax.ppermute(pair, 'rows', [(0, 2), (2, 0), (1, 3), (3, 1)])  18.9 us
    ppermute x16, starting transfers between devices, go_right(): return lax.ppermute(x, 'chan', self.right)  17.2 us
    ppermute x16, starting transfers between devices, go_left(): return lax.ppermute(x, 'chan', self.left)  16.7 us
  transfers between devices with their start and end apart: 62, of which 35 were waited for; matrix products, arithmetic and copies ran while one was open for 16% of the time, Pallas kernels for 4%

profile of v1, /device:TPU:0, one launch (start us, length us, event | category | flops | bytes accessed | tf_op | source)
XLA Modules:
  0.0 386.2 jit_solution(9541808590218619837)
XLA Ops:
  9.2 6.0 %collective-permute-done.refs_1_ = bf16[160,1536]{1,0:T(8,128)(2,1)S(1)} collective-permute-done((bf16[160,1536]{1,0:T(8,128)(2,1)}, bf16[160,1536]{1,0:T(8,128)(2,1)S(1)}, u32[]{:S(2)}, u32[]{:S(2)}) %collective-permute-start) | collective-permute-done | bytes 491552 | tf_op jit(solution)/shard_map/ppermute | solution.py:348
  19.1 10.3 %collective-permute-done.5 = f32[2,7,192]{2,1,0:T(8,128)S(1)} collective-permute-done((f32[2,7,192]{2,1,0:T(8,128)S(1)}, f32[2,7,192]{2,1,0:T(8,128)S(1)}, u32[]{:S(2)}, u32[]{:S(2)}) %collective-permute-start.5) | collective-permute-done | bytes 10784 | tf_op jit(solution)/shard_map/ppermute | solution.py:446
  32.6 8.4 %collective-permute-done.7.refs_5_ = bf16[160,1536]{1,0:T(8,128)(2,1)S(1)} collective-permute-done((bf16[160,1536]{1,0:T(8,128)(2,1)S(1)}, bf16[160,1536]{1,0:T(8,128)(2,1)S(1)}, u32[]{:S(2)}, u32[]{:S(2)}) %collective-permute-start.7) | collective-permute-done | bytes 491552 | tf_op jit(solution)/shard_map/ppermute | solution.py:348
  43.3 4.0 %collective-permute-done.9 = bf16[80,1536]{1,0:T(8,128)(2,1)S(1)} collective-permute-done((bf16[80,1536]{1,0:T(8,128)(2,1)S(1)}, bf16[80,1536]{1,0:T(8,128)(2,1)S(1)}, u32[]{:S(2)}, u32[]{:S(2)}) %collective-permute-start.9) | collective-permute-done | bytes 245792 | tf_op jit(solution)/shard_map/ppermute | solution.py:348
  57.3 4.6 %collective-permute-done.6 = f32[4,7,192]{2,1,0:T(8,128)S(1)} collective-permute-done((f32[4,7,192]{2,1,0:T(8,128)S(1)}, f32[4,7,192]{2,1,0:T(8,128)S(1)}, u32[]{:S(2)}, u32[]{:S(2)}) %collective-permute-start.6) | collective-permute-done | bytes 21536 | tf_op jit(solution)/shard_map/ppermute | solution.py:446
  66.2 6.3 %place_norm.1 = (bf16[1280,1536]{1,0:T(8,128)(2,1)S(1)}, bf16[1280,1536]{1,0:T(8,128)(2,1)S(1)}) custom-call(s32[8]{0:T(128)S(1)} %stack.68.owners_ref, s32[1,2]{1,0:T(1,128)S(1)} %bitcast_subtract_fusion.begins_ref, f32[8,1536]{1,0:T(8,128)S(1)} %pad.18.mod_ref, bf16[160,1536]{1,0:T(8,128)(2,1)S(1)} %copy-done.6, bf16[160,1536]{1,0:T(8,128)(2,1)S(1)} %copy-done.17, ...), custom_call_target="tpu_custom_call" | custom-call | flops 39321600 | bytes 11796480 | tf_op jit(solution)/shard_map/place_norm/pallas_call | solution.py:538
  75.6 3.4 multiply_convert_fusion
  82.4 3.4 collective-permute-done.13
  85.8 5.9 %collective-permute-done.15.refs_4_ = bf16[160,1536]{1,0:T(8,128)(2,1)S(1)} collective-permute-done((bf16[160,1536]{1,0:T(8,128)(2,1)}, bf16[160,1536]{1,0:T(8,128)(2,1)S(1)}, u32[]{:S(2)}, u32[]{:S(2)}) %collective-permute-start.15) | collective-permute-done | bytes 491552 | tf_op jit(solution)/shard_map/ppermute | solution.py:351
  101.1 4.5 %collective-permute-done.17 = bf16[160,128]{1,0:T(8,128)(2,1)S(1)} collective-permute-done((bf16[160,128]{1,0:T(8,128)(2,1)S(1)}, bf16[160,128]{1,0:T(8,128)(2,1)S(1)}, u32[]{:S(2)}, u32[]{:S(2)}) %collective-permute-start.17) | collective-permute-done | bytes 40992 | tf_op jit(solution)/shard_map/ppermute | solution.py:420
  113.0 5.9 %fusion.37.z_ref = f32[1280,384]{1,0:T(8,128)} fusion(bf16[1280,1536]{1,0:T(8,128)(2,1)} %copy-done.24, bf16[384,1536]{1,0:T(8,128)(2,1)} %param.24), kind=kOutput, calls=%fused_computation.182 | convolution fusion | flops 1509949440 | bytes 7077888 | tf_op jit(solution)/shard_map/dot_general | solution.py:285
  128.6 3.7 place_gate.1
  132.4 3.8 fusion.38.d_gated_ref
  137.1 74.8 %scan_all.1 = (bf16[1280,384]{1,0:T(8,128)(2,1)}, bf16[1280,384]{1,0:T(8,128)(2,1)}, bf16[1280,384]{1,0:T(8,128)(2,1)}, f32[1280,384]{1,0:T(8,128)}, f32[16,384]...) custom-call(s32[1,2]{1,0:T(1,128)} %copy-done.22, bf16[1280,128]{1,0:T(8,128)(2,1)} %pad_maximum_fusion.5.proj_ref, ...), custom_call_target="tpu_custom_call" | custom-call | flops 471859200 | bytes 11796480 | tf_op jit(solution)/shard_map/scan_all/pallas_call | solution.py:238
  211.9 3.6 convolution_convert_fusion.branch_ref
  228.1 4.0 %collective-permute-done.25 = bf16[80,1536]{1,0:T(8,128)(2,1)S(1)} collective-permute-done((bf16[80,1536]{1,0:T(8,128)(2,1)S(1)}, bf16[80,1536]{1,0:T(8,128)(2,1)S(1)}, u32[]{:S(2)}, u32[]{:S(2)}) %collective-permute-start.25) | collective-permute-done | bytes 245792 | tf_op jit(solution)/shard_map/ppermute | solution.py:348
  239.8 4.2 %collective-permute-done.36 = bf16[160,128]{1,0:T(8,128)(2,1)S(1)} collective-permute-done((bf16[160,128]{1,0:T(8,128)(2,1)S(1)}, bf16[160,128]{1,0:T(8,128)(2,1)S(1)}, u32[]{:S(2)}, u32[]{:S(2)}) %collective-permute-start.36) | collective-permute-done | bytes 40992 | tf_op jit(solution)/shard_map/ppermute | solution.py:420
  251.1 4.7 %collective-permute-done.38 = bf16[640,128]{1,0:T(8,128)(2,1)S(1)} collective-permute-done((bf16[640,128]{1,0:T(8,128)(2,1)S(1)}, bf16[640,128]{1,0:T(8,128)(2,1)S(1)}, u32[]{:S(2)}, u32[]{:S(2)}) %collective-permute-start.38) | collective-permute-done | bytes 163872 | tf_op jit(solution)/shard_map/ppermute | solution.py:420
  268.2 6.7 %collective-permute-done.31 = bf16[160,1536]{1,0:T(8,128)(2,1)S(1)} collective-permute-done((bf16[160,1536]{1,0:T(8,128)(2,1)S(1)}, bf16[160,1536]{1,0:T(8,128)(2,1)S(1)}, u32[]{:S(2)}, u32[]{:S(2)}) %collective-permute-start.31) | collective-permute-done | bytes 491552 | tf_op jit(solution)/shard_map/ppermute | solution.py:351
  280.5 4.6 %collective-permute-done.32 = bf16[160,1536]{1,0:T(8,128)(2,1)S(1)} collective-permute-done((bf16[160,1536]{1,0:T(8,128)(2,1)S(1)}, bf16[160,1536]{1,0:T(8,128)(2,1)S(1)}, u32[]{:S(2)}, u32[]{:S(2)}) %collective-permute-start.32) | collective-permute-done | bytes 491552 | tf_op jit(solution)/shard_map/ppermute | solution.py:351
  311.8 5.3 %token_sums.1 = f32[8,1536]{1,0:T(8,128)S(1)} custom-call(s32[1,2]{1,0:T(1,128)S(1)} %copy-done.23, bf16[1280,1536]{1,0:T(8,128)(2,1)S(1)} %copy-done.3, bf16[1280,1536]{1,0:T(8,128)(2,1)S(1)} %copy-done.9, bf16[1280,1536]{1,0:T(8,128)(2,1)S(1)} %copy-done.11, bf16[1280,1536]{1,0:T(8,128)(2,1)S(1)} %copy-done.5), custom_call_target="tpu_custom_call" | custom-call | flops 23592960 | bytes 15728640 | tf_op jit(solution)/shard_map/token_sums/pallas_call | solution.py:588
  324.3 15.6 %collective-permute-done.46 = bf16[384,1536]{1,0:T(8,128)(2,1)} collective-permute-done((bf16[384,1536]{1,0:T(8,128)(2,1)S(1)}, bf16[384,1536]{1,0:T(8,128)(2,1)}, u32[]{:S(2)}, u32[]{:S(2)}) %collective-permute-start.46) | collective-permute-done | bytes 1179680 | tf_op jit(solution)/shard_map/ppermute | solution.py:470
  339.9 4.5 %convert_add_fusion.1 = (f32[384,1536]{1,0:T(8,128)}, f32[384,1536]{1,0:T(8,128)}) fusion(bf16[384,1536]{1,0:T(8,128)(2,1)} %collective-permute-done.46, bf16[384,1536]{1,0:T(8,128)(2,1)S(1)} %add_convert_fusion.1, bf16[384,1536]{1,0:T(8,128)(2,1)} %collective-permute-done.44, bf16[384,1536]{1,0:T(8,128)(2,1)S(1)} %add_convert_fusion.2), kind=kLoop, calls=%fused_computation.5 | loop fusion | flops 3538944 | bytes 9437184 | tf_op jit(solution)/shard_map/add | solution.py:472
  382.4 3.4 fusion.15
  (379 shorter events, 182.2 us)
Async XLA Ops:
  0.7 14.5 %collective-permute-start = (bf16[160,1536]{1,0:T(8,128)(2,1)}, bf16[160,1536]{1,0:T(8,128)(2,1)S(1)}, u32[]{:S(2)}, u32[]{:S(2)}) collective-permute-start(bf16[160,1536]{1,0:T(8,128)(2,1)} %refs_0_.1), channel_id=1, source_target_pairs={{0,2},{2,4},{4,6},{6,7},{7,5},{5,3},{3,1},{1,0},{8,10},{10,12},{12... | collective-permute-start | bytes 1474568 | tf_op jit(solution)/shard_map/ppermute | solution.py:348
  3.8 13.2 %collective-permute-start.2 = (bf16[160,1536]{1,0:T(8,128)(2,1)}, bf16[160,1536]{1,0:T(8,128)(2,1)}, u32[]{:S(2)}, u32[]{:S(2)}) collective-permute-start(bf16[160,1536]{1,0:T(8,128)(2,1)} %refs_0_.1), channel_id=1, source_target_pairs={{2,0},{4,2},{6,4},{7,6},{5,7},{3,5},{1,3},{0,1},{10,8},{12,10},{14... | collective-permute-start | bytes 1474568 | tf_op jit(solution)/shard_map/ppermute | solution.py:351
  15.2 14.2 %collective-permute-start.1 = (bf16[160,1536]{1,0:T(8,128)(2,1)S(1)}, bf16[160,1536]{1,0:T(8,128)(2,1)S(1)}, u32[]{:S(2)}, u32[]{:S(2)}) collective-permute-start(bf16[160,1536]{1,0:T(8,128)(2,1)S(1)} %collective-permute-done.refs_1_), channel_id=1, source_target_pairs={{0,2},{2,4},{4,6},{6,7},{7,5},{5,3},{3,1},{1,0},{8,10},{10,12},{12... | collective-permute-start | bytes 1474568 | tf_op jit(solution)/shard_map/ppermute | solution.py:348
  16.9 12.5 %collective-permute-start.3 = (bf16[160,1536]{1,0:T(8,128)(2,1)}, bf16[160,1536]{1,0:T(8,128)(2,1)S(1)}, u32[]{:S(2)}, u32[]{:S(2)}) collective-permute-start(bf16[160,1536]{1,0:T(8,128)(2,1)} %collective-permute-done.2.refs_2_), channel_id=1, source_target_pairs={{2,0},{4,2},{6,4},{7,6},{5,7},{3,5},{1,3},{0,1},{10,8},{12,10},{14... | collective-permute-start | bytes 1474568 | tf_op jit(solution)/shard_map/ppermute | solution.py:351
  17.3 12.2 %collective-permute-start.5 = (f32[2,7,192]{2,1,0:T(8,128)S(1)}, f32[2,7,192]{2,1,0:T(8,128)S(1)}, u32[]{:S(2)}, u32[]{:S(2)}) collective-permute-start(f32[2,7,192]{2,1,0:T(8,128)S(1)} %pad_maximum_fusion.13), channel_id=1, source_target_pairs={{0,2},{1,3},{2,0},{3,1},{4,6},{5,7},{6,4},{7,5},{8,10},{9,11},{10,... | collective-permute-start | bytes 32264 | tf_op jit(solution)/shard_map/ppermute | solution.py:446
  49.7 22.8 %collective-permute-start.12 = (bf16[160,1536]{1,0:T(8,128)(2,1)S(1)}, bf16[160,1536]{1,0:T(8,128)(2,1)}, u32[]{:S(2)}, u32[]{:S(2)}) collective-permute-start(bf16[160,1536]{1,0:T(8,128)(2,1)S(1)} %copy-done.12), channel_id=1, source_target_pairs={{2,0},{4,2},{6,4},{7,6},{5,7},{3,5},{1,3},{0,1},{10,8},{12,10},{14... | collective-permute-start | bytes 1474568 | tf_op jit(solution)/shard_map/ppermute | solution.py:351
  50.8 21.7 %collective-permute-start.11 = (bf16[160,1536]{1,0:T(8,128)(2,1)S(1)}, bf16[160,1536]{1,0:T(8,128)(2,1)}, u32[]{:S(2)}, u32[]{:S(2)}) collective-permute-start(bf16[160,1536]{1,0:T(8,128)(2,1)S(1)} %copy-done.12), channel_id=1, source_target_pairs={{0,2},{2,4},{4,6},{6,7},{7,5},{5,3},{3,1},{1,0},{8,10},{10,12},{12... | collective-permute-start | bytes 1474568 | tf_op jit(solution)/shard_map/ppermute | solution.py:348
  82.0 11.9 %collective-permute-start.14 = (bf16[160,1536]{1,0:T(8,128)(2,1)}, bf16[160,1536]{1,0:T(8,128)(2,1)S(1)}, u32[]{:S(2)}, u32[]{:S(2)}) collective-permute-start(bf16[160,1536]{1,0:T(8,128)(2,1)} %collective-permute-done.11.refs_1_), channel_id=1, source_target_pairs={{0,2},{2,4},{4,6},{6,7},{7,5},{5,3},{3,1},{1,0},{8,10},{10,12},{12... | collective-permute-start | bytes 1474568 | tf_op jit(solution)/shard_map/ppermute | solution.py:348
  82.3 12.4 %collective-permute-start.56 = (bf16[1,2,1536]{2,1,0:T(2,128)(2,1)S(1)}, bf16[1,2,1536]{2,1,0:T(2,128)(2,1)S(1)}, u32[]{:S(2)}, u32[]{:S(2)}) collective-permute-start(bf16[1,2,1536]{2,1,0:T(2,128)(2,1)S(1)} %bitcast.92), channel_id=1, source_target_pairs={{0,8},{8,0},{16,24},{24,16},{1,9},{9,1},{17,25},{25,17},{2,10},{10... | collective-permute-start | bytes 18440 | tf_op jit(solution)/shard_map/ppermute | solution.py:446
  122.5 13.8 %collective-permute-start.22 = (bf16[640,128]{1,0:T(8,128)(2,1)S(1)}, bf16[640,128]{1,0:T(8,128)(2,1)S(1)}, u32[]{:S(2)}, u32[]{:S(2)}) collective-permute-start(bf16[640,128]{1,0:T(8,128)(2,1)S(1)} %pad_maximum_fusion.7), channel_id=1, source_target_pairs={{0,1},{1,0},{2,3},{3,2},{4,5},{5,4},{6,7},{7,6},{8,9},{9,8},{10,11... | collective-permute-start | bytes 491528 | tf_op jit(solution)/shard_map/ppermute | solution.py:420
  234.2 14.4 %collective-permute-start.30 = (bf16[160,1536]{1,0:T(8,128)(2,1)S(1)}, bf16[160,1536]{1,0:T(8,128)(2,1)S(1)}, u32[]{:S(2)}, u32[]{:S(2)}) collective-permute-start(bf16[160,1536]{1,0:T(8,128)(2,1)S(1)} %pad_maximum_fusion.2), channel_id=1, source_target_pairs={{2,0},{4,2},{6,4},{7,6},{5,7},{3,5},{1,3},{0,1},{10,8},{12,10},{14... | collective-permute-start | bytes 1474568 | tf_op jit(solution)/shard_map/ppermute | solution.py:351
  246.0 43.3 %collective-permute-start.45 = (f32[384,1536]{1,0:T(8,128)S(1)}, f32[384,1536]{1,0:T(8,128)S(1)}, u32[]{:S(2)}, u32[]{:S(2)}) collective-permute-start(f32[384,1536]{1,0:T(8,128)S(1)} %fusion.41), channel_id=1, source_target_pairs={{0,8},{8,0},{16,24},{24,16},{1,9},{9,1},{17,25},{25,17},{2,10},{10... | collective-permute-start | bytes 7077896 | tf_op jit(solution)/shard_map/ppermute | solution.py:467
  246.0 41.2 %collective-permute-start.43 = (f32[384,1536]{1,0:T(8,128)S(1)}, f32[384,1536]{1,0:T(8,128)S(1)}, u32[]{:S(2)}, u32[]{:S(2)}) collective-permute-start(f32[384,1536]{1,0:T(8,128)S(1)} %fusion.40), channel_id=1, source_target_pairs={{0,8},{8,0},{16,24},{24,16},{1,9},{9,1},{17,25},{25,17},{2,10},{10... | collective-permute-start | bytes 7077896 | tf_op jit(solution)/shard_map/ppermute | solution.py:467
  250.8 12.6 %collective-permute-start.27 = (bf16[160,1536]{1,0:T(8,128)(2,1)S(1)}, bf16[160,1536]{1,0:T(8,128)(2,1)S(1)}, u32[]{:S(2)}, u32[]{:S(2)}) collective-permute-start(bf16[160,1536]{1,0:T(8,128)(2,1)S(1)} %add_convert_fusion.11), channel_id=1, source_target_pairs={{0,2},{2,4},{4,6},{6,7},{7,5},{5,3},{3,1},{1,0},{8,10},{10,12},{12... | collective-permute-start | bytes 1474568 | tf_op jit(solution)/shard_map/ppermute | solution.py:348
  266.7 57.6 %collective-permute-start.58 = (f32[384,1536]{1,0:T(8,128)}, f32[384,1536]{1,0:T(8,128)}, u32[]{:S(2)}, u32[]{:S(2)}) collective-permute-start(f32[384,1536]{1,0:T(8,128)} %fusion.42), channel_id=1, source_target_pairs={{0,8},{8,0},{16,24},{24,16},{1,9},{9,1},{17,25},{25,17},{2,10},{10... | collective-permute-start | bytes 7077896 | tf_op jit(solution)/shard_map/ppermute | solution.py:467
  266.8 13.7 %collective-permute-start.28 = (bf16[160,1536]{1,0:T(8,128)(2,1)S(1)}, bf16[160,1536]{1,0:T(8,128)(2,1)S(1)}, u32[]{:S(2)}, u32[]{:S(2)}) collective-permute-start(bf16[160,1536]{1,0:T(8,128)(2,1)S(1)} %get-tuple-element.200), channel_id=1, source_target_pairs={{0,2},{2,4},{4,6},{6,7},{7,5},{5,3},{3,1},{1,0},{8,10},{10,12},{12... | collective-permute-start | bytes 1474568 | tf_op jit(solution)/shard_map/ppermute | solution.py:348
  287.8 36.5 %collective-permute-start.44 = (bf16[384,1536]{1,0:T(8,128)(2,1)S(1)}, bf16[384,1536]{1,0:T(8,128)(2,1)}, u32[]{:S(2)}, u32[]{:S(2)}) collective-permute-start(bf16[384,1536]{1,0:T(8,128)(2,1)S(1)} %add_convert_fusion.2), channel_id=1, source_target_pairs={{0,16},{16,0},{8,24},{24,8},{1,17},{17,1},{9,25},{25,9},{2,18},{18... | collective-permute-start | bytes 3538952 | tf_op jit(solution)/shard_map/ppermute | solution.py:470
  296.6 43.3 %collective-permute-start.46 = (bf16[384,1536]{1,0:T(8,128)(2,1)S(1)}, bf16[384,1536]{1,0:T(8,128)(2,1)}, u32[]{:S(2)}, u32[]{:S(2)}) collective-permute-start(bf16[384,1536]{1,0:T(8,128)(2,1)S(1)} %add_convert_fusion.1), channel_id=1, source_target_pairs={{0,16},{16,0},{8,24},{24,8},{1,17},{17,1},{9,25},{25,9},{2,18},{18... | collective-permute-start | bytes 3538952 | tf_op jit(solution)/shard_map/ppermute | solution.py:470
  298.2 19.0 %collective-permute-start.40 = (bf16[160,1536]{1,0:T(8,128)(2,1)}, bf16[160,1536]{1,0:T(8,128)(2,1)}, u32[]{:S(2)}, u32[]{:S(2)}) collective-permute-start(bf16[160,1536]{1,0:T(8,128)(2,1)} %pad_maximum_fusion.3), channel_id=1, source_target_pairs={{0,2},{2,4},{4,6},{6,7},{7,5},{5,3},{3,1},{1,0},{8,10},{10,12},{12... | collective-permute-start | bytes 1474568 | tf_op jit(solution)/shard_map/ppermute | solution.py:348
  298.3 20.9 %collective-permute-start.42 = (bf16[160,1536]{1,0:T(8,128)(2,1)}, bf16[160,1536]{1,0:T(8,128)(2,1)S(1)}, u32[]{:S(2)}, u32[]{:S(2)}) collective-permute-start(bf16[160,1536]{1,0:T(8,128)(2,1)} %pad_maximum_fusion.4), channel_id=1, source_target_pairs={{2,0},{4,2},{6,4},{7,6},{5,7},{3,5},{1,3},{0,1},{10,8},{12,10},{14... | collective-permute-start | bytes 1474568 | tf_op jit(solution)/shard_map/ppermute | solution.py:351
  321.3 35.5 %collective-permute-start.52 = (f32[8,1536]{1,0:T(8,128)S(1)}, f32[8,1536]{1,0:T(8,128)S(1)}, u32[]{:S(2)}, u32[]{:S(2)}) collective-permute-start(f32[8,1536]{1,0:T(8,128)S(1)} %add.660), channel_id=1, source_target_pairs={{0,2},{1,3},{2,0},{3,1},{4,6},{5,7},{6,4},{7,5},{8,10},{9,11},{10,... | collective-permute-start | bytes 147464 | tf_op jit(solution)/shard_map/ppermute | solution.py:457
  322.5 28.2 %collective-permute-start.61 = (f32[256,384]{1,0:T(8,128)S(1)}, f32[256,384]{1,0:T(8,128)S(1)}, u32[]{:S(2)}, u32[]{:S(2)}) collective-permute-start(f32[256,384]{1,0:T(8,128)S(1)} %add.669), channel_id=1, source_target_pairs={{0,16},{16,0},{8,24},{24,8},{1,17},{17,1},{9,25},{25,9},{2,18},{18... | collective-permute-start | bytes 1179656 | tf_op jit(solution)/shard_map/ppermute | solution.py:470
  349.1 20.2 %collective-permute-start.59 = (bf16[384,1536]{1,0:T(8,128)(2,1)S(1)}, bf16[384,1536]{1,0:T(8,128)(2,1)S(1)}, u32[]{:S(2)}, u32[]{:S(2)}) collective-permute-start(bf16[384,1536]{1,0:T(8,128)(2,1)S(1)} %add_convert_fusion), channel_id=1, source_target_pairs={{0,16},{16,0},{8,24},{24,8},{1,17},{17,1},{9,25},{25,9},{2,18},{18... | collective-permute-start | bytes 3538952 | tf_op jit(solution)/shard_map/ppermute | solution.py:470
  356.9 18.0 %collective-permute-start.53 = (f32[8,1536]{1,0:T(8,128)S(1)}, f32[8,1536]{1,0:T(8,128)}, u32[]{:S(2)}, u32[]{:S(2)}) collective-permute-start(f32[8,1536]{1,0:T(8,128)S(1)} %add.661), channel_id=1, source_target_pairs={{0,4},{1,5},{2,6},{3,7},{4,0},{5,1},{6,2},{7,3},{8,12},{9,13},{10,... | collective-permute-start | bytes 147464 | tf_op jit(solution)/shard_map/ppermute | solution.py:457
  (102 other events, 1153.9 us)
